TPU v7x, 512 devices: a whole 4x4x16 slice. The times are simulated.
512 devices in a mesh: ctx: 64 (over y, z_lo, x), isl: 8 (over z_hi, core).
Axes of the slice: x: 4, y: 4, z: 16 (z_hi: 4, z_lo: 4; z = z_hi * 4 + z_lo), core: 2. Of those that a mesh axis runs over, the one named last changes fastest.
Arguments:
- layer_input: bfloat16 [8, 16384, 4096], P('isl', 'ctx'), may hold values from -6 to 6
- queries: bfloat16 [8, 16384, 1024], P('isl', 'ctx'), may hold values from -110 to 110
- grad_out: bfloat16 [8, 16384, 1024], P('isl', 'ctx'), may hold values from -6 to 6
- key_weight: bfloat16 [4096, 128], P(('ctx', 'isl')), may hold values from -0.09375 to 0.09375
- value_weight: bfloat16 [4096, 128], P(('ctx', 'isl')), may hold values from -0.09375 to 0.09375
- doc_len: int32 [8, 85], P('isl'), may hold values from 1 to 8, 256 in all within a row
Outputs:
- attn_out: bfloat16 [8, 16384, 1024], P('isl', 'ctx')
- grad_queries: bfloat16 [8, 16384, 1024], P('isl', 'ctx')
- grad_key_weight: float32 [4096, 128], P(('ctx', 'isl'))
- grad_value_weight: float32 [4096, 128], P(('ctx', 'isl'))
Inputs may be any that keep to these rules, and one draw needn't show every extreme that they name: `doc_len`: lengths in units of 64 tokens; those of one sequence sum to 256, and the longest of each sequence is exactly 8.
All inputs are finite; a program needn't handle non-finite values.
Results may differ from a plain program's by a relative error of at most 0.034.
The roundings to bfloat16 on the way count: a program that leaves them out, or rounds other values in their place, can miss the bound.
Values may be sent and summed in bfloat16 or wider, within the bound.
No kernel may reach another device: no remote copies, remote signals or barrier semaphores. Data moves between devices by JAX's collectives and lax.ppermute only.
A program may use at most 64 MiB of HBM per device.

v0:
```python
import jax
import jax.numpy as jnp
from jax import lax
from jax.sharding import PartitionSpec as P

HD = 128
QPK = 8
GROUPS = 1


far_limit = 2**30
last_dims = (((1,), (1,)), ((), ()))
first_dims = (((0,), (0,)), ((), ()))


def document_owners(lengths, owners, capacity):
    count = lengths.shape[0]
    numbers = jnp.arange(count, dtype=jnp.int32)
    ranking = jnp.argsort(-(lengths * count + (count - 1 - numbers)))
    ordered = jnp.take(lengths, ranking)
    places = jnp.arange(owners, dtype=jnp.int32)

    def place(carry, length):
        load, filled = carry
        fits = filled + length <= capacity
        score = jnp.where(fits, load * owners + places, far_limit)
        winner = jnp.argmin(score)
        chosen = places == winner
        begin = jnp.sum(jnp.where(chosen, filled, 0))
        load = load + jnp.where(chosen, length * (length + 1) // 2, 0)
        filled = filled + jnp.where(chosen, length, 0)
        return ((load, filled), (winner, begin))

    empty = jnp.zeros((owners,), jnp.int32)
    unused, (winners, begins) = lax.scan(place, (empty, empty), ordered)
    owner_of = jnp.zeros((count,), jnp.int32).at[ranking].set(winners)
    first_of = jnp.zeros((count,), jnp.int32).at[ranking].set(begins)
    return (owner_of, first_of)


def routing(lengths, owners, capacity, rows):
    owner_of, first_of = document_owners(lengths, owners, capacity)
    ends = jnp.cumsum(lengths)
    begins = ends - lengths
    numbers = jnp.arange(lengths.shape[0], dtype=jnp.int32)
    places = jnp.arange(owners, dtype=jnp.int32)
    slots = jnp.arange(capacity, dtype=jnp.int32)
    shifted = slots[None, :, None] - first_of[None, None, :]
    hits = (
        (owner_of[None, None, :] == places[:, None, None])
        & (shifted >= 0)
        & (shifted < lengths[None, None, :])
    )
    filled = jnp.any(hits, axis=2)
    slot_unit = jnp.sum(jnp.where(hits, begins[None, None, :] + shifted, 0), axis=2)
    slot_doc = jnp.where(filled, jnp.sum(jnp.where(hits, numbers[None, None, :], 0), axis=2), -1)
    units = jnp.arange(rows, dtype=jnp.int32)
    inside = (units[:, None] >= begins[None, :]) & (units[:, None] < ends[None, :])
    offset = owner_of * capacity + first_of - begins
    unit_place = jnp.sum(jnp.where(inside, offset[None, :], 0), axis=1) + units
    return (filled, slot_unit, slot_doc, unit_place)


def pack(rows_array, slot_unit, filled):
    width = rows_array.shape[1]
    picked = jnp.take(rows_array, slot_unit.reshape(-1), axis=0).reshape(slot_unit.shape + (width,))
    return jnp.where(filled[..., None], picked, jnp.zeros((), rows_array.dtype))


def to_rows(array):
    return array.transpose(1, 0, 2).reshape(-1, array.shape[2])


def to_slots(array, owners):
    return array.reshape(-1, owners, array.shape[1]).transpose(1, 0, 2)


def project(inputs, key_weight, value_weight):
    key_part = jnp.dot(
        inputs,
        lax.all_gather(key_weight, ("ctx", "isl"), axis=0, tiled=True),
        preferred_element_type=jnp.float32,
    )
    value_part = jnp.dot(
        inputs,
        lax.all_gather(value_weight, ("ctx", "isl"), axis=0, tiled=True),
        preferred_element_type=jnp.float32,
    )
    return (key_part.astype(jnp.bfloat16), value_part.astype(jnp.bfloat16))


def softmax_rows(scores):
    peak = jnp.max(scores, axis=1, keepdims=True)
    expo = jnp.exp(scores - peak)
    return expo / jnp.sum(expo, axis=1, keepdims=True)


def head_slices(queries, keys, values, grads, head):
    group = head // QPK
    query = lax.dynamic_slice_in_dim(queries, head * HD, HD, 1)
    grad = lax.dynamic_slice_in_dim(grads, head * HD, HD, 1)
    return (group, query, grad, keys, values)


def write_heads(carry, head, output, dquery, dkey, dvalue):
    outputs, dqueries, dkeys, dvalues = carry
    outputs = lax.dynamic_update_slice_in_dim(outputs, output, head * HD, 1)
    dqueries = lax.dynamic_update_slice_in_dim(dqueries, dquery, head * HD, 1)
    old_keys = dkeys
    old_values = dvalues
    dkeys = old_keys + dkey
    dvalues = old_values + dvalue
    return (outputs, dqueries, dkeys, dvalues)


def start_heads(queries, keys):
    return (
        jnp.zeros(queries.shape, jnp.bfloat16),
        jnp.zeros(queries.shape, jnp.bfloat16),
        jnp.zeros(keys.shape, jnp.float32),
        jnp.zeros(keys.shape, jnp.float32),
    )


def dense_pass(queries, keys, values, grads, allowed):
    scale = float(HD) ** (-0.5)

    def head_step(head, carry):
        group, query, grad, key, value = head_slices(queries, keys, values, grads, head)
        scores = lax.dot_general(query, key, last_dims, preferred_element_type=jnp.float32) * scale
        probs = softmax_rows(jnp.where(allowed, scores, -jnp.inf))
        probs_low = probs.astype(jnp.bfloat16)
        output = jnp.dot(probs_low, value, preferred_element_type=jnp.float32).astype(jnp.bfloat16)
        delta = jnp.sum(
            grad.astype(jnp.float32) * output.astype(jnp.float32), axis=1, keepdims=True
        )
        dprobs = lax.dot_general(grad, value, last_dims, preferred_element_type=jnp.float32)
        dscores = (probs * (dprobs - delta)).astype(jnp.bfloat16)
        dquery = (jnp.dot(dscores, key, preferred_element_type=jnp.float32) * scale).astype(
            jnp.bfloat16
        )
        dkey = (
            lax.dot_general(dscores, query, first_dims, preferred_element_type=jnp.float32) * scale
        )
        dvalue = lax.dot_general(probs_low, grad, first_dims, preferred_element_type=jnp.float32)
        return write_heads(carry, head, output, dquery, dkey, dvalue)

    outputs, dqueries, dkeys, dvalues = lax.fori_loop(
        0, GROUPS * QPK, head_step, start_heads(queries, keys)
    )
    return (outputs, dqueries, dkeys.astype(jnp.bfloat16), dvalues.astype(jnp.bfloat16))


def per_device(layer_input, queries, grad_out, key_weight, value_weight, doc_len):
    inputs = layer_input[0]
    query_rows = queries[0]
    grad_rows = grad_out[0]
    owners = lax.axis_size("ctx")
    rows = inputs.shape[0]
    capacity = 2 * rows // owners
    filled, slot_unit, slot_doc, unit_place = routing(doc_len[0], owners, capacity, rows)
    key_rows, value_rows = project(inputs, key_weight, value_weight)
    sent = (
        pack(query_rows, slot_unit, filled),
        pack(key_rows, slot_unit, filled),
        pack(value_rows, slot_unit, filled),
        pack(grad_rows, slot_unit, filled),
    )
    got_queries, got_keys, got_values, got_grads = (
        lax.all_to_all(sent[0], "ctx", split_axis=0, concat_axis=0, tiled=True),
        lax.all_to_all(sent[1], "ctx", split_axis=0, concat_axis=0, tiled=True),
        lax.all_to_all(sent[2], "ctx", split_axis=0, concat_axis=0, tiled=True),
        lax.all_to_all(sent[3], "ctx", split_axis=0, concat_axis=0, tiled=True),
    )
    own_doc = jnp.take(slot_doc, lax.axis_index("ctx"), axis=0)
    row_doc = jnp.repeat(own_doc, owners)
    numbers = jnp.arange(row_doc.shape[0], dtype=jnp.int32)
    row_doc = jnp.where(row_doc >= 0, row_doc, -1 - numbers)
    allowed = (row_doc[:, None] == row_doc[None, :]) & (numbers[None, :] <= numbers[:, None])
    owned = (to_rows(got_queries), to_rows(got_keys), to_rows(got_values), to_rows(got_grads))
    outputs, dqueries, dkeys, dvalues = dense_pass(owned[0], owned[1], owned[2], owned[3], allowed)
    returned = (
        to_slots(outputs, owners),
        to_slots(dqueries, owners),
        to_slots(dkeys, owners),
        to_slots(dvalues, owners),
    )
    back = (
        lax.all_to_all(returned[0], "ctx", split_axis=0, concat_axis=0, tiled=True),
        lax.all_to_all(returned[1], "ctx", split_axis=0, concat_axis=0, tiled=True),
        lax.all_to_all(returned[2], "ctx", split_axis=0, concat_axis=0, tiled=True),
        lax.all_to_all(returned[3], "ctx", split_axis=0, concat_axis=0, tiled=True),
    )
    mine = [jnp.take(part.reshape(-1, part.shape[2]), unit_place, axis=0) for part in back]
    key_grad = lax.dot_general(inputs, mine[2], first_dims, preferred_element_type=jnp.float32)
    value_grad = lax.dot_general(inputs, mine[3], first_dims, preferred_element_type=jnp.float32)
    key_share, value_share = (
        lax.psum_scatter(key_grad, ("ctx", "isl"), scatter_dimension=0, tiled=True),
        lax.psum_scatter(value_grad, ("ctx", "isl"), scatter_dimension=0, tiled=True),
    )
    return (mine[0][None], mine[1][None], key_share, value_share)


def solution(mesh):
    placed = (
        P("isl", "ctx", None),
        P("isl", "ctx", None),
        P("isl", "ctx", None),
        P(("ctx", "isl"), None),
        P(("ctx", "isl"), None),
        P("isl", None),
    )
    return jax.shard_map(
        per_device,
        mesh=mesh,
        in_specs=placed,
        out_specs=(
            P("isl", "ctx", None),
            P("isl", "ctx", None),
            P(("ctx", "isl"), None),
            P(("ctx", "isl"), None),
        ),
        check_vma=False,
    )
```

profile of v0, /device:TPU:2, one launch (start us, length us, event | category | flops | bytes accessed | tf_op | source)
XLA Modules:
  0.0 2291.4 jit_solution(11442229636193482724)
XLA Ops:
  9.4 2.6 sort.17
  13.5 560.4 %while.44 = (s32[]{:T(128)}, s32[64]{0:T(128)S(1)}, s32[64]{0:T(128)S(1)}, s32[85]{0:T(128)S(1)}, s32[85]{0:T(128)S(1)}, /*index=5*/s32[85]{0:T(128)S(1)}) while((s32[]{:T(128)}, s32[64]{0:T(128)S(1)}, s32[64]{0:T(128)S(1)}, s32[85]{0:T(128)S(1)}, s32[85]{0:T(128)S(1)}, /*index=5*/s32[85]{0:T(128)S(1)}) %tuple.111), condition=%wide.region_4.5_spmd.clone.clone.clone, body=%wide.region_1.0_spmd.clone.clone.sunk.clone | while | flops 1484 | bytes 1862 | solution.py:35
  16.7 1.9 fusion.121
  23.3 1.9 fusion.121
  29.9 1.9 fusion.121
  43.1 1.9 fusion.121
  49.7 1.9 fusion.121
  56.3 1.9 fusion.121
  62.9 1.9 fusion.121
  69.5 1.9 fusion.121
  76.1 1.9 fusion.121
  82.7 1.9 fusion.121
  89.3 1.9 fusion.121
  95.9 1.9 fusion.121
  102.5 1.9 fusion.121
  109.0 1.9 fusion.121
  115.6 1.9 fusion.121
  122.2 1.9 fusion.121
  128.8 1.9 fusion.121
  142.0 1.9 fusion.121
  214.5 1.9 fusion.121
  578.5 2.2 select_reduce_fusion
  582.0 181.6 %all-gather.5.cloned.1.call-done = bf16[4096,128]{1,0:T(8,128)(2,1)} async-done(((bf16[8,128]{1,0:T(8,128)(2,1)}), bf16[4096,128]{1,0:T(8,128)(2,1)}) %all-gather.5.cloned.1.call-update) | async-done | bytes 1048592 | tf_op jit(solution)/shard_map/all_gather | solution.py:86
  763.6 1.9 fusion.33
  766.9 739.6 %all-gather.3.cloned.1.call-done = bf16[4096,128]{1,0:T(8,128)(2,1)} async-done(((bf16[8,128]{1,0:T(8,128)(2,1)}), bf16[4096,128]{1,0:T(8,128)(2,1)}) %all-gather.3.cloned.1.call-update) | async-done | bytes 1048592 | tf_op jit(solution)/shard_map/all_gather | solution.py:81
  1506.5 1.9 fusion.30
  1510.6 15.7 all_to_all.40
  1526.3 5.8 all-to-all-start.2
  1532.1 2.8 gather_fusion.4
  1534.9 2.8 gather_fusion.1
  1537.7 2.9 bitcast_select_fusion
  1541.8 36.9 %all_to_all.41 = bf16[64,8,1024]{2,1,0:T(8,128)(2,1)} all-to-all(bf16[64,8,1024]{2,1,0:T(8,128)(2,1)S(1)} %get-tuple-element.489), channel_id=1, replica_groups=mesh['ctx'=64,'isl'=8] {'ctx'}, dimensions={0} | all-to-all | bytes 2097152 | tf_op jit(solution)/shard_map/all_to_all | solution.py:170
  1578.7 5.9 all-to-all-start.3
  1587.8 2.8 copy.70
  1590.6 21.8 all-to-all-done.3
  1616.2 97.5 %while.43 = (s32[]{:T(128)}, bf16[512,1024]{1,0:T(8,128)(2,1)}, bf16[512,1024]{1,0:T(8,128)(2,1)}, f32[512,128]{1,0:T(8,128)S(1)}, f32[512,128]{1,0:T(8,128)}, /...) while((s32[]{:T(128)}, bf16[512,1024]{1,0:T(8,128)(2,1)}, ...), condition=%wide.region_15.18_spmd.clone.clone, body=%wide.region_11.17_spmd.clone.sunk.clone | while | flops 407632384 | bytes 15112462 | solution.py:148
  1623.4 1.9 fusion.119
  1634.7 2.0 fusion.119
  1637.9 2.0 convolution_add_fusion.3
  1647.1 1.9 fusion.119
  1650.2 2.0 convolution_add_fusion.3
  1659.4 1.9 fusion.119
  1662.5 2.0 convolution_add_fusion.3
  1671.7 1.9 fusion.119
  1674.8 2.0 convolution_add_fusion.3
  1683.9 1.9 fusion.119
  1687.1 2.0 convolution_add_fusion.3
  1696.2 1.9 fusion.119
  1699.4 2.0 convolution_add_fusion.3
  1708.6 1.9 fusion.119
  1711.8 2.0 convolution_add_fusion.3
  1714.5 5.9 all-to-all-start.6
  1722.2 8.0 all-to-all-done.6
  1730.2 5.5 all-to-all-start.7
  1735.7 2.8 copy.94
  1738.5 7.0 all-to-all-done.7
  1745.5 5.5 all-to-all-start.5
  1751.1 2.9 copy.77
  1753.9 23.0 %all-to-all-done.5 = bf16[64,8,1024]{2,1,0:T(8,128)(2,1)S(1)} async-done(((bf16[64,8,1024]{2,1,0:T(8,128)(2,1)}), bf16[64,8,1024]{2,1,0:T(8,128)(2,1)S(1)}, u32[]{:S(2)}, u32[]{:S(2)}) %all-to-all-start.5) | async-done | bytes 1048608 | tf_op jit(solution)/shard_map/all_to_all | solution.py:190
  1776.9 6.3 all-to-all-start.4
  1787.3 1.9 convolution_bitcast_fusion
  1789.2 487.3 %all-reduce.5.cloned.1.call-done = (f32[4096,128]{0,1:T(8,128)}, f32[4096,128]{0,1:T(8,128)}) async-done(((f32[4096,128]{0,1:T(8,128)}, f32[4096,128]{0,1:T(8,128)}), (f32[4096,128]{0,1:T(8,128)}, f32[4096,128]{0,1:T(8,128)})) %all-reduce.5.cloned.1.call-update) | async-done | bytes 4194320
  2278.8 2.0 gather_fusion.6
  2280.7 3.0 gather_fusion.5
  (611 shorter events, 511.0 us)
Async XLA Ops:
  7.2 756.5 %copy-start = (bf16[1,256,4096]{2,1,0:T(8,128)(2,1)S(1)}, bf16[1,256,4096]{2,1,0:T(8,128)(2,1)}, u32[]{:S(2)}) copy-start(bf16[1,256,4096]{2,1,0:T(8,128)(2,1)} %param.18) | copy-start | bytes 6291460
  7.2 756.5 %all-gather.5.cloned.1.call-start = ((), (), s32[]{:S(2)}) async-start(), calls=%async_computation.9 | async-start | bytes 1050624 | tf_op jit(solution)/shard_map/all_gather | solution.py:86
  7.9 1498.6 %all-gather.3.cloned.1.call-start = ((), (), s32[]{:S(2)}) async-start(), calls=%async_computation.8 | async-start | bytes 1050624 | tf_op jit(solution)/shard_map/all_gather | solution.py:81
  766.9 765.2 %copy-start.2 = (bf16[1,256,1024]{2,1,0:T(8,128)(2,1)S(1)}, bf16[1,256,1024]{2,1,0:T(8,128)(2,1)}, u32[]{:S(2)}) copy-start(bf16[1,256,1024]{2,1,0:T(8,128)(2,1)} %param.20) | copy-start | bytes 1572868
  1526.3 15.5 all-to-all-start.2
  1532.1 2.8 copy-start.3
  1541.8 36.9 %copy-start.6 = (bf16[64,8,128]{2,1,0:T(8,128)(2,1)}, bf16[64,8,128]{2,1,0:T(8,128)(2,1)S(1)}, u32[]{:S(2)}) copy-start(bf16[64,8,128]{2,1,0:T(8,128)(2,1)S(1)} %all-to-all-done.2) | copy-start | bytes 393220
  1578.7 33.7 %all-to-all-start.3 = ((bf16[64,8,1024]{2,1,0:T(8,128)(2,1)}), bf16[64,8,1024]{2,1,0:T(8,128)(2,1)S(1)}, u32[]{:S(2)}, u32[]{:S(2)}) async-start(bf16[64,8,1024]{2,1,0:T(8,128)(2,1)} %get-tuple-element.488), calls=%async_computation.3 | async-start | bytes 2097152 | tf_op jit(solution)/shard_map/all_to_all | solution.py:173
  1616.2 3.5 copy-start.7
  1618.6 1.0 copy-start.4
  1623.4 4.2 copy-start.8
  1627.6 3.5 copy-start.7
  1629.9 1.0 copy-start.4
  1634.7 5.2 copy-start.8
  1639.9 3.5 copy-start.7
  1642.2 1.0 copy-start.4
  1647.0 5.2 copy-start.8
  1652.2 3.5 copy-start.7
  1654.6 1.0 copy-start.4
  1659.3 5.2 copy-start.8
  1664.5 3.5 copy-start.7
  1666.9 1.0 copy-start.4
  1671.6 5.2 copy-start.8
  1676.8 3.5 copy-start.7
  1679.2 1.0 copy-start.4
  1683.9 5.2 copy-start.8
  1689.1 3.5 copy-start.7
  1691.4 1.0 copy-start.4
  1696.2 5.2 copy-start.8
  1701.4 3.5 copy-start.7
  1703.7 1.0 copy-start.4
  1708.6 5.2 copy-start.8
  1714.5 15.6 all-to-all-start.6
  1730.2 15.3 all-to-all-start.7
  1745.5 31.4 %all-to-all-start.5 = ((bf16[64,8,1024]{2,1,0:T(8,128)(2,1)}), bf16[64,8,1024]{2,1,0:T(8,128)(2,1)S(1)}, u32[]{:S(2)}, u32[]{:S(2)}) async-start(bf16[64,8,1024]{2,1,0:T(8,128)(2,1)} %bitcast.137), calls=%async_computation.5 | async-start | bytes 2097152 | tf_op jit(solution)/shard_map/all_to_all | solution.py:190
  1751.0 32.5 %copy-start.1 = (s32[1,85]{1,0:T(1,128)S(1)}, s32[1,85]{1,0:T(1,128)}, u32[]{:S(2)}) copy-start(s32[1,85]{1,0:T(1,128)} %param.23) | copy-start | bytes 1024
  1751.0 32.5 %copy-start.9 = (s32[85]{0:T(128)S(1)}, s32[85]{0:T(128)}, u32[]{:S(2)}) copy-start(s32[85]{0:T(128)} %get-tuple-element.479) | copy-start | bytes 1024
  1776.9 503.8 %all-to-all-start.4 = ((bf16[64,8,1024]{2,1,0:T(8,128)(2,1)}), bf16[64,8,1024]{2,1,0:T(8,128)(2,1)}, u32[]{:S(2)}, u32[]{:S(2)}) async-start(bf16[64,8,1024]{2,1,0:T(8,128)(2,1)} %copy.77), calls=%async_computation.4 | async-start | bytes 2097152 | tf_op jit(solution)/shard_map/all_to_all | solution.py:189
  1783.2 493.2 %all-reduce.5.cloned.1.call-start = ((), (), s32[]{:S(2)}) async-start(), calls=%async_computation.10 | async-start | bytes 8388608
  2280.7 3.0 copy-start.5
Sparse Core Ops, SparseCore 0:
  10.1 753.4 all-gather.4
  765.8 740.6 all-gather.2
  1789.5 486.8 all-reduce.4
where the time goes:
time: 2300 us; the launch traced here: 2290 us
  waiting for transfers between devices  1470 us (64%)
  other arithmetic  291 us (13%)
  local copies, waits for them, and re-layouts  234 us (10%)
  loops' own time  113 us (5%)
  matrix products  80.7 us (4%)
  blocking collectives  52.6 us (2%)
  starting transfers between devices  35.4 us (2%)
    all_gather x1, waiting for transfers between devices, project(): lax.all_gather(key_weight, ('ctx', 'isl'), axis=0, tiled=True)  740 us
    unnamed x4, waiting for transfers between devices  489 us
    all_gather x1, waiting for transfers between devices, project(): lax.all_gather(value_weight, ('ctx', 'isl'), axis=0, tiled=True)  182 us
    reduce_sum x85, other arithmetic, place(): begin = jnp.sum(jnp.where(chosen, filled, 0))  162 us
    dynamic_update_slice x170, local copies, waits for them, and re-layouts, document_owners(): unused, (winners, begins) = lax.scan(place, (empty, empty), ordered)  126 us
    another operation x1, loops' own time, document_owners(): unused, (winners, begins) = lax.scan(place, (empty, empty), ordered)  112 us
    another operation x85, other arithmetic, place(): winner = jnp.argmin(score)  111 us
    dynamic_slice x85, local copies, waits for them, and re-layouts, document_owners(): unused, (winners, begins) = lax.scan(place, (empty, empty), ordered)  49.5 us
  transfers between devices with their start and end apart: 9, of which 8 were waited for; matrix products, arithmetic and copies ran while one was open for 22% of the time, Pallas kernels for 0%

commit v1 on v0

v1 whole, which is shorter than its diff:
```python
import math

import jax
import jax.numpy as jnp
from jax import lax
from jax.experimental import pallas as pl
from jax.experimental.pallas import tpu as pltpu
from jax.sharding import Mesh, PartitionSpec as P

HD = 128
QPK = 8
WIDTH = QPK * HD
COLS = 64
OWN = 4
BLOCKS = 3

SPLIT = ("y", "zl", "x", "zh", "core")
CTX = ("y", "zl", "x")
PLANE = ("y", "x")
LINE = ("zl", "zh")
last_dims = (((1,), (1,)), ((), ()))
plain_dims = (((1,), (0,)), ((), ()))
first_dims = (((0,), (0,)), ((), ()))
hidden = -1e30


def attention_kernel(begin_ref, first_ref, got_ref, back_ref, bias_ref, p_ref, ds_ref):
    rows = got_ref.shape[0]
    keys = BLOCKS * rows
    first = first_ref[0]
    scale = float(HD) ** -0.5
    factor = scale * math.log2(math.e)

    key_row = lax.broadcasted_iota(jnp.int32, (keys, 1), 0)
    key_block = key_row // rows
    key_col = (key_row - key_block * rows) // OWN
    key_unit = first + (key_block - (BLOCKS - 1)) * OWN + key_row % OWN
    key_pos = key_unit * COLS + key_col
    row = lax.broadcasted_iota(jnp.int32, (1, rows), 1)
    slot = row % OWN
    row_pos = (first + slot) * COLS + row // OWN
    start = jnp.zeros((1, rows), jnp.int32)
    for i in range(OWN):
        start = jnp.where(slot == i, begin_ref[i], start)
    allowed = (key_unit >= start) & (key_pos <= row_pos)
    bias_ref[...] = jnp.where(allowed, 0.0, hidden).astype(jnp.float32)

    def window(place):
        parts = [got_ref[:, 2 * WIDTH + (2 * k + place) * HD:][:, :HD] for k in range(BLOCKS)]
        return jnp.concatenate(parts, axis=0)

    key, value = window(0), window(1)
    key_t, value_t = key.T, value.T
    for head in range(QPK):
        cols = slice(head * HD, (head + 1) * HD)
        gcols = slice(WIDTH + head * HD, WIDTH + (head + 1) * HD)
        part = slice(head * rows, (head + 1) * rows)
        query = got_ref[:, cols]
        grad = got_ref[:, gcols]
        grad_t = grad.T.astype(jnp.float32)
        score = lax.dot_general(key, query, last_dims, preferred_element_type=jnp.float32)
        score = score * factor + bias_ref[...]
        expo = jnp.exp2(score - jnp.max(score, axis=0, keepdims=True))
        probs = expo * (1.0 / jnp.sum(expo, axis=0, keepdims=True))
        low = probs.astype(jnp.bfloat16)
        p_ref[:, part] = low
        out_t = lax.dot_general(value_t, low, plain_dims, preferred_element_type=jnp.float32)
        out_t = out_t.astype(jnp.bfloat16)
        back_ref[:, cols] = out_t.T
        delta = jnp.sum(grad_t * out_t.astype(jnp.float32), axis=0, keepdims=True)
        dprobs = lax.dot_general(value, grad, last_dims, preferred_element_type=jnp.float32)
        dscore = (probs * (dprobs - delta)).astype(jnp.bfloat16)
        ds_ref[:, part] = dscore
        dq_t = lax.dot_general(key_t, dscore, plain_dims, preferred_element_type=jnp.float32) * scale
        back_ref[:, gcols] = dq_t.astype(jnp.bfloat16).T
    for k in range(BLOCKS):
        block = slice(k * rows, (k + 1) * rows)
        dkey = jnp.zeros((rows, HD), jnp.float32)
        dvalue = jnp.zeros((rows, HD), jnp.float32)
        for head in range(QPK):
            cols = slice(head * HD, (head + 1) * HD)
            gcols = slice(WIDTH + head * HD, WIDTH + (head + 1) * HD)
            part = slice(head * rows, (head + 1) * rows)
            dkey += lax.dot_general(ds_ref[block, part], got_ref[:, cols], plain_dims, preferred_element_type=jnp.float32)
            dvalue += lax.dot_general(p_ref[block, part], got_ref[:, gcols], plain_dims, preferred_element_type=jnp.float32)
        at = 2 * WIDTH + 2 * k * HD
        back_ref[:, at:at + HD] = (dkey * scale).astype(jnp.bfloat16)
        back_ref[:, at + HD:at + 2 * HD] = dvalue.astype(jnp.bfloat16)


def attention(begins, first, got):
    rows = got.shape[0]
    keys = BLOCKS * rows
    vmem = pl.BlockSpec(memory_space=pltpu.VMEM)
    smem = pl.BlockSpec(memory_space=pltpu.SMEM)
    return pl.pallas_call(
        attention_kernel,
        out_shape=jax.ShapeDtypeStruct(got.shape, jnp.bfloat16),
        in_specs=[smem, smem, vmem],
        out_specs=vmem,
        scratch_shapes=[
            pltpu.VMEM((keys, rows), jnp.float32),
            pltpu.VMEM((keys, QPK * rows), jnp.bfloat16),
            pltpu.VMEM((keys, QPK * rows), jnp.bfloat16),
        ],
        compiler_params=pltpu.CompilerParams(vmem_limit_bytes=40 * 1024 * 1024),
        cost_estimate=pl.CostEstimate(
            flops=10 * rows * keys * HD * QPK, bytes_accessed=4 * got.size, transcendentals=rows * keys * QPK
        ),
    )(begins, first, got)


def exchange(array, axes):
    return lax.all_to_all(array, axes, split_axis=0, concat_axis=0, tiled=True)


def spread(array, axes):
    count = lax.axis_size(axes)
    return exchange(jnp.broadcast_to(array[None], (count,) + array.shape), axes)


def swap(array):
    return lax.ppermute(array, "core", [(0, 1), (1, 0)])


def later(array, steps):
    fill = jnp.zeros((steps, array.shape[1]), array.dtype)
    return jnp.concatenate([fill, array[:-steps]], axis=0)


def earlier(array, steps):
    fill = jnp.zeros((steps, array.shape[1]), array.dtype)
    return jnp.concatenate([array[steps:], fill], axis=0)


def gather_weights(weight):
    line = spread(weight, LINE)
    plane = spread(line, PLANE)
    other = swap(plane)
    core = lax.axis_index("core")
    both = jnp.where(core == 0, jnp.stack([plane, other]), jnp.stack([other, plane]))
    rows, width = weight.shape
    natural = both.reshape(2, 4, 4, 4, 4, rows, width).transpose(1, 3, 2, 4, 0, 5, 6)
    return natural.reshape(-1, width)


def reduce_weights(part):
    width = part.shape[1]
    rows = part.shape[0] // 512
    split = part.reshape(4, 4, 4, 4, 2, rows, width).transpose(4, 0, 2, 1, 3, 5, 6)
    core = jnp.sum(exchange(split.reshape(2, -1, width), "core"), axis=0)
    plane = jnp.sum(exchange(core.reshape(16, -1, width), PLANE), axis=0)
    return jnp.sum(exchange(plane.reshape(16, rows, width), LINE), axis=0)


def per_device(layer_input, queries, grad_out, key_weight, value_weight, doc_len):
    inputs = layer_input[0]
    place = lax.axis_index(CTX)
    ends = jnp.cumsum(doc_len[0])
    units = place * OWN + jnp.arange(OWN, dtype=jnp.int32)
    begins = jnp.max(jnp.where(ends[None, :] <= units[:, None], ends[None, :], 0), axis=1)
    first = (place * OWN).astype(jnp.int32).reshape(1)

    weight = gather_weights(jnp.concatenate([key_weight, value_weight], axis=1))
    kv = jnp.dot(inputs, weight, preferred_element_type=jnp.float32).astype(jnp.bfloat16)
    window = [kv if k == 0 else later(kv, k * OWN) for k in reversed(range(BLOCKS))]
    sent = jnp.concatenate([queries[0], grad_out[0]] + window, axis=1)
    got = exchange(sent, CTX)

    back = exchange(attention(begins, first, got), CTX)

    parts = [back[:, 2 * WIDTH + 2 * k * HD:][:, :2 * HD].astype(jnp.float32) for k in range(BLOCKS)]
    dkv = parts[BLOCKS - 1]
    for k in range(1, BLOCKS):
        dkv = dkv + earlier(parts[BLOCKS - 1 - k], k * OWN)
    grad = lax.dot_general(inputs, dkv.astype(jnp.bfloat16), first_dims, preferred_element_type=jnp.float32)
    share = reduce_weights(grad)
    return (back[None, :, :WIDTH], back[None, :, WIDTH:2 * WIDTH], share[:, :HD], share[:, HD:])


def solution(mesh):
    split = Mesh(mesh.devices.reshape(4, 4, 4, 4, 2), SPLIT)
    isl = ("zh", "core")
    placed = (
        P(isl, CTX, None),
        P(isl, CTX, None),
        P(isl, CTX, None),
        P(SPLIT, None),
        P(SPLIT, None),
        P(isl, None),
    )
    return jax.shard_map(
        per_device,
        mesh=split,
        in_specs=placed,
        out_specs=(
            P(isl, CTX, None),
            P(isl, CTX, None),
            P(SPLIT, None),
            P(SPLIT, None),
        ),
        check_vma=False,
    )
```

time: 2300 us -> 254 us (0.11)
  the two profiles are of different devices: /device:TPU:2 before, /device:TPU:32 now
where the time goes in v1:
time: 254 us; the launch traced here: 253 us
  blocking collectives  135 us (53%)
  waiting for transfers between devices  47.8 us (19%)
  local copies, waits for them, and re-layouts  30.2 us (12%)
  starting transfers between devices  14.2 us (6%)
  Pallas kernels  10.8 us (4%)
  other arithmetic  10.5 us (4%)
  matrix products  3.42 us (1%)
    all_to_all x5, blocking collectives, exchange(): return lax.all_to_all(array, axes, split_axis=0, concat_axis=0, tiled=True)  135 us
    all_to_all x2, waiting for transfers between devices, exchange(): return lax.all_to_all(array, axes, split_axis=0, concat_axis=0, tiled=True)  47.8 us
    all_to_all x2, starting transfers between devices, exchange(): return lax.all_to_all(array, axes, split_axis=0, concat_axis=0, tiled=True)  12.3 us
    pallas_call x1, Pallas kernels, attention(): pl.pallas_call(attention_kernel, out_shape=jax.ShapeDtypeStruct(got.shape...  10.8 us
    all_to_all x3, local copies, waits for them, and re-layouts, exchange(): return lax.all_to_all(array, axes, split_axis=0, concat_axis=0, tiled=True)  7.96 us
    unnamed x10, local copies, waits for them, and re-layouts  6.73 us
    dot_general x1, local copies, waits for them, and re-layouts, per_device(): lax.dot_general(inputs, dkv.astype(jnp.bfloat16), first_dims, preferred_e...  5.6 us
  transfers between devices with their start and end apart: 3, of which 2 were waited for; matrix products, arithmetic and copies ran while one was open for 4% of the time, Pallas kernels for 0%

profile of v1, /device:TPU:32, one launch (start us, length us, event | category | flops | bytes accessed | tf_op | source)
XLA Modules:
  0.0 253.2 jit_solution(16883019193162646807)
XLA Ops:
  0.6 0.0 copy-start
  0.6 0.8 pad_maximum_fusion
  1.5 27.2 %all_to_all.45 = bf16[16,8,256]{2,1,0:T(8,128)(2,1)S(1)} all-to-all(bf16[16,8,256]{2,1,0:T(8,128)(2,1)S(1)} %broadcast_in_dim.19), channel_id=1, replica_groups=mesh['y'=4,'zl'=4,'x'=4,'zh'=4,'core'=2] {'zl','zh'}, dimensions={0} | all-to-all | bytes 131072 | tf_op jit(solution)/shard_map/all_to_all | solution.py:114
  28.7 0.1 broadcast_in_dim.20
  28.8 23.1 %all_to_all.46 = bf16[16,16,8,256]{3,2,1,0:T(8,128)(2,1)S(1)} all-to-all(bf16[16,16,8,256]{3,2,1,0:T(8,128)(2,1)S(1)} %broadcast_in_dim.20), channel_id=1, replica_groups=mesh['y'=4,'zl'=4,'x'=4,'zh'=4,'core'=2] {'y','x'}, dimensions={0} | all-to-all | bytes 2097152 | tf_op jit(solution)/shard_map/all_to_all | solution.py:114
  51.9 1.9 collective-permute-start
  53.8 2.0 concatenate.35
  55.8 2.0 concatenate.36
  57.8 2.1 constant_dynamic-update-slice_fusion.4
  59.9 2.1 constant_dynamic-update-slice_fusion.3
  62.0 0.0 collective-permute-done
  62.0 1.9 fusion
  63.9 0.2 copy.19
  64.0 0.0 copy-done
  64.0 0.7 fusion.7
  64.9 0.0 copy-start.2
  65.0 0.7 constant_dynamic-update-slice_fusion.2
  65.7 0.7 constant_dynamic-update-slice_fusion.1
  66.5 0.7 constant_dynamic-update-slice_fusion
  67.2 5.3 %all-to-all-start.2 = ((bf16[64,4,2816]{2,1,0:T(4,128)(2,1)}), bf16[64,4,2816]{2,1,0:T(4,128)(2,1)}, u32[]{:S(2)}, u32[]{:S(2)}) async-start(bf16[64,4,2816]{2,1,0:T(4,128)(2,1)} %constant_dynamic-update-slice_fusion), calls=%async_computation.2 | async-start | bytes 2883584 | tf_op jit(solution)/shard_map/all_to_all | solution.py:114
  72.6 0.0 copy-done.2
  72.6 0.1 copy.18
  72.7 0.1 reduce-window.8
  72.8 0.1 reduce
  72.9 0.2 select_reduce_fusion.begin_ref
  73.1 34.7 %all-to-all-done.2 = bf16[64,4,2816]{2,1,0:T(4,128)(2,1)} async-done(((bf16[64,4,2816]{2,1,0:T(4,128)(2,1)}), bf16[64,4,2816]{2,1,0:T(4,128)(2,1)}, u32[]{:S(2)}, u32[]{:S(2)}) %all-to-all-start.2) | async-done | bytes 1441824 | tf_op jit(solution)/shard_map/all_to_all | solution.py:114
  107.8 2.6 %all_to_all.31.got_ref = bf16[256,2816]{1,0:T(8,128)(2,1)S(1)} reshape(bf16[64,4,2816]{2,1,0:T(4,128)(2,1)} %all-to-all-done.2) | data formatting | bytes 2883584 | tf_op jit(solution)/shard_map/all_to_all | solution.py:114
  110.4 10.8 %shard_map.93 = bf16[256,2816]{1,0:T(8,128)(2,1)S(1)} custom-call(s32[4]{0:T(128)S(1)} %select_reduce_fusion.begin_ref, s32[1]{0:T(128)} %bitcast.1.first_ref, bf16[256,2816]{1,0:T(8,128)(2,1)S(1)} %all_to_all.31.got_ref), custom_call_target="tpu_custom_call" | custom-call | flops 2013265920 | bytes 2883584 | tf_op jit(solution)/shard_map/pallas_call | solution.py:96
  121.2 0.0 copy-start.1
  121.2 1.1 copy-done.1
  122.3 2.7 %all_to_all.32 = bf16[64,4,2816]{2,1,0:T(4,128)(2,1)S(1)} reshape(bf16[256,2816]{1,0:T(8,128)(2,1)} %copy-done.1) | data formatting | bytes 2883584 | tf_op jit(solution)/shard_map/all_to_all | solution.py:114
  125.1 42.9 %all_to_all.47 = bf16[64,4,2816]{2,1,0:T(4,128)(2,1)} all-to-all(bf16[64,4,2816]{2,1,0:T(4,128)(2,1)S(1)} %all_to_all.32), channel_id=1, replica_groups=mesh['y'=4,'zl'=4,'x'=4,'zh'=4,'core'=2] {'y','zl','x'}, dimensions={0} | all-to-all | bytes 2883584 | tf_op jit(solution)/shard_map/all_to_all | solution.py:114
  168.0 2.6 %all_to_all.34 = bf16[256,2816]{1,0:T(8,128)(2,1)S(1)} reshape(bf16[64,4,2816]{2,1,0:T(4,128)(2,1)} %all_to_all.47) | data formatting | bytes 2883584 | tf_op jit(solution)/shard_map/all_to_all | solution.py:114
  170.6 2.7 %convolution_bitcast_fusion = f32[4096,256]{0,1:T(8,128)} fusion(bf16[1,256,4096]{2,1,0:T(8,128)(2,1)S(1)} %copy-done, bf16[256,2816]{1,0:T(8,128)(2,1)S(1)} %all_to_all.34, bf16[248,256]{1,0:T(8,128)(2,1)S(1)} %slice.52, bf16[252,256]{1,0:T(8,128)(2,1)S(1)} %slice.51), kind=kOutput, calls=%fused_computation | convolution fusion | flops 537264128 | bytes 6680576 | tf_op jit(solution)/shard_map/dot_general | solution.py:176
  173.3 5.6 %copy.20 = f32[4096,256]{1,0:T(8,128)} copy(f32[4096,256]{0,1:T(8,128)} %convolution_bitcast_fusion) | data formatting | bytes 8388608 | tf_op jit(solution)/shard_map/dot_general | solution.py:176
  178.9 2.8 %copy.21 = f32[2,4,4,4,4,8,256]{6,5,4,3,2,1,0:T(8,128)S(1)} copy(f32[2,4,4,4,4,8,256]{6,5,0,4,2,3,1:T(8,128)} %bitcast.32) | data formatting | bytes 8388608 | tf_op jit(solution)/shard_map/transpose | solution.py:150
  181.8 8.2 %all_to_all.48 = f32[2,2048,256]{2,1,0:T(8,128)} all-to-all(f32[2,2048,256]{2,1,0:T(8,128)S(1)} %bitcast.33), channel_id=1, replica_groups=mesh['y'=4,'zl'=4,'x'=4,'zh'=4,'core'=2] {'core'}, dimensions={0} | all-to-all | bytes 8388608 | tf_op jit(solution)/shard_map/all_to_all | solution.py:114
  189.9 4.0 %reduce_sum.27 = f32[2048,256]{1,0:T(8,128)} reduce(f32[2,2048,256]{2,1,0:T(8,128)} %all_to_all.48, f32[]{:T(128)} %constant.35.clone.1), dimensions={0}, to_apply=%region_2.3 | reduce | flops 524288 | bytes 6291460 | tf_op jit(solution)/shard_map/reduce_sum | solution.py:151
  194.0 34.2 %all_to_all.49 = f32[16,128,256]{2,1,0:T(8,128)} all-to-all(f32[16,128,256]{2,1,0:T(8,128)} %bitcast.34), channel_id=1, replica_groups=mesh['y'=4,'zl'=4,'x'=4,'zh'=4,'core'=2] {'y','x'}, dimensions={0} | all-to-all | bytes 4194304 | tf_op jit(solution)/shard_map/all_to_all | solution.py:114
  228.2 2.4 reduce_sum.28
  230.5 6.9 %all-to-all-start.6 = ((f32[16,8,256]{2,1,0:T(8,128)}), f32[16,8,256]{2,1,0:T(8,128)}, u32[]{:S(2)}, u32[]{:S(2)}) async-start(f32[16,8,256]{2,1,0:T(8,128)} %bitcast.38), calls=%async_computation.6 | async-start | bytes 262144 | tf_op jit(solution)/shard_map/all_to_all | solution.py:114
  237.4 1.1 slice_bitcast_fusion
  238.6 13.1 %all-to-all-done.6 = f32[16,8,256]{2,1,0:T(8,128)} async-done(((f32[16,8,256]{2,1,0:T(8,128)}), f32[16,8,256]{2,1,0:T(8,128)}, u32[]{:S(2)}, u32[]{:S(2)}) %all-to-all-start.6) | async-done | bytes 131104 | tf_op jit(solution)/shard_map/all_to_all | solution.py:114
  251.7 0.9 reduce_sum.29
  252.6 0.6 fusion.14
  (10 shorter events, 0.2 us)
Async XLA Ops:
  0.6 63.4 %copy-start = (bf16[1,256,4096]{2,1,0:T(8,128)(2,1)S(1)}, bf16[1,256,4096]{2,1,0:T(8,128)(2,1)}, u32[]{:S(2)}) copy-start(bf16[1,256,4096]{2,1,0:T(8,128)(2,1)} %param.6) | copy-start | bytes 6291460
  51.9 10.1 %collective-permute-start = (bf16[16,16,8,256]{3,2,1,0:T(8,128)(2,1)S(1)}, bf16[16,16,8,256]{3,2,1,0:T(8,128)(2,1)}, u32[]{:S(2)}, u32[]{:S(2)}) collective-permute-start(bf16[16,16,8,256]{3,2,1,0:T(8,128)(2,1)S(1)} %all_to_all.46), channel_id=1, source_target_pairs={{0,1},{1,0},{2,3},{3,2},{4,5},{5,4},{6,7},{7,6},{8,9},{9,8},{10,11... | collective-permute-start | bytes 3145736 | tf_op jit(solution)/shard_map/ppermute | solution.py:123
  64.9 7.7 %copy-start.2 = (s32[1,85]{1,0:T(1,128)S(1)}, s32[1,85]{1,0:T(1,128)}, u32[]{:S(2)}) copy-start(s32[1,85]{1,0:T(1,128)} %param.11) | copy-start | bytes 1024
  67.2 40.6 %all-to-all-start.2 = ((bf16[64,4,2816]{2,1,0:T(4,128)(2,1)}), bf16[64,4,2816]{2,1,0:T(4,128)(2,1)}, u32[]{:S(2)}, u32[]{:S(2)}) async-start(bf16[64,4,2816]{2,1,0:T(4,128)(2,1)} %constant_dynamic-update-slice_fusion), calls=%async_computation.2 | async-start | bytes 2883584 | tf_op jit(solution)/shard_map/all_to_all | solution.py:114
  121.2 1.1 copy-start.1
  230.5 21.2 %all-to-all-start.6 = ((f32[16,8,256]{2,1,0:T(8,128)}), f32[16,8,256]{2,1,0:T(8,128)}, u32[]{:S(2)}, u32[]{:S(2)}) async-start(f32[16,8,256]{2,1,0:T(8,128)} %bitcast.38), calls=%async_computation.6 | async-start | bytes 262144 | tf_op jit(solution)/shard_map/all_to_all | solution.py:114

commit v2 on v1

v2 whole, which is shorter than its diff:
```python
import math

import jax
import jax.numpy as jnp
from jax import lax
from jax.experimental import pallas as pl
from jax.experimental.pallas import tpu as pltpu
from jax.sharding import Mesh, PartitionSpec as P

HD = 128
QPK = 8
WIDTH = QPK * HD
COLS = 64
OWN = 4
BLOCKS = 3

SPLIT = ("y", "zl", "x", "zh", "core")
CTX = ("y", "zl", "x")
PLANE = ("y", "x")
LINE = ("zl", "zh")
last_dims = (((1,), (1,)), ((), ()))
plain_dims = (((1,), (0,)), ((), ()))
first_dims = (((0,), (0,)), ((), ()))
hidden = -1e30
FEATURES = 2 * WIDTH + 2 * BLOCKS * HD
vmem = pl.BlockSpec(memory_space=pltpu.VMEM)
smem = pl.BlockSpec(memory_space=pltpu.SMEM)
roomy = pltpu.CompilerParams(vmem_limit_bytes=40 * 1024 * 1024)


def attention_kernel(begin_ref, first_ref, sent_ref, back_ref, got_ref, bias_ref, p_ref, ds_ref):
    rows = COLS * OWN
    keys = BLOCKS * rows
    first = first_ref[0]
    got_ref[...] = sent_ref[...].reshape(rows, FEATURES)
    scale = float(HD) ** -0.5
    factor = scale * math.log2(math.e)

    key_row = lax.broadcasted_iota(jnp.int32, (keys, 1), 0)
    key_block = key_row // rows
    key_col = (key_row - key_block * rows) // OWN
    key_unit = first + (key_block - (BLOCKS - 1)) * OWN + key_row % OWN
    key_pos = key_unit * COLS + key_col
    row = lax.broadcasted_iota(jnp.int32, (1, rows), 1)
    slot = row % OWN
    row_pos = (first + slot) * COLS + row // OWN
    start = jnp.zeros((1, rows), jnp.int32)
    for i in range(OWN):
        start = jnp.where(slot == i, begin_ref[i], start)
    allowed = (key_unit >= start) & (key_pos <= row_pos)
    bias_ref[...] = jnp.where(allowed, 0.0, hidden).astype(jnp.float32)

    def window(place):
        parts = [got_ref[:, 2 * WIDTH + (2 * k + place) * HD:][:, :HD] for k in range(BLOCKS)]
        return jnp.concatenate(parts, axis=0)

    key, value = window(0), window(1)
    key_t, value_t = key.T, value.T
    for head in range(QPK):
        cols = slice(head * HD, (head + 1) * HD)
        gcols = slice(WIDTH + head * HD, WIDTH + (head + 1) * HD)
        part = slice(head * rows, (head + 1) * rows)
        query = got_ref[:, cols]
        grad = got_ref[:, gcols]
        grad_t = grad.T.astype(jnp.float32)
        score = lax.dot_general(key, query, last_dims, preferred_element_type=jnp.float32)
        score = score * factor + bias_ref[...]
        expo = jnp.exp2(score - jnp.max(score, axis=0, keepdims=True))
        probs = expo * (1.0 / jnp.sum(expo, axis=0, keepdims=True))
        low = probs.astype(jnp.bfloat16)
        p_ref[:, part] = low
        out_t = lax.dot_general(value_t, low, plain_dims, preferred_element_type=jnp.float32)
        out_t = out_t.astype(jnp.bfloat16)
        back_ref[:, :, cols] = out_t.T.reshape(COLS, OWN, HD)
        delta = jnp.sum(grad_t * out_t.astype(jnp.float32), axis=0, keepdims=True)
        dprobs = lax.dot_general(value, grad, last_dims, preferred_element_type=jnp.float32)
        dscore = (probs * (dprobs - delta)).astype(jnp.bfloat16)
        ds_ref[:, part] = dscore
        dq_t = lax.dot_general(key_t, dscore, plain_dims, preferred_element_type=jnp.float32) * scale
        back_ref[:, :, gcols] = dq_t.astype(jnp.bfloat16).T.reshape(COLS, OWN, HD)
    for k in range(BLOCKS):
        block = slice(k * rows, (k + 1) * rows)
        dkey = jnp.zeros((rows, HD), jnp.float32)
        dvalue = jnp.zeros((rows, HD), jnp.float32)
        for head in range(QPK):
            cols = slice(head * HD, (head + 1) * HD)
            gcols = slice(WIDTH + head * HD, WIDTH + (head + 1) * HD)
            part = slice(head * rows, (head + 1) * rows)
            dkey += lax.dot_general(ds_ref[block, part], got_ref[:, cols], plain_dims, preferred_element_type=jnp.float32)
            dvalue += lax.dot_general(p_ref[block, part], got_ref[:, gcols], plain_dims, preferred_element_type=jnp.float32)
        at = 2 * WIDTH + 2 * k * HD
        back_ref[:, :, at:at + HD] = (dkey * scale).astype(jnp.bfloat16).reshape(COLS, OWN, HD)
        back_ref[:, :, at + HD:at + 2 * HD] = dvalue.astype(jnp.bfloat16).reshape(COLS, OWN, HD)


def attention(begins, first, sent):
    rows = COLS * OWN
    keys = BLOCKS * rows
    return pl.pallas_call(
        attention_kernel,
        out_shape=jax.ShapeDtypeStruct(sent.shape, jnp.bfloat16),
        in_specs=[smem, smem, vmem],
        out_specs=vmem,
        scratch_shapes=[
            pltpu.VMEM((rows, FEATURES), jnp.bfloat16),
            pltpu.VMEM((keys, rows), jnp.float32),
            pltpu.VMEM((keys, QPK * rows), jnp.bfloat16),
            pltpu.VMEM((keys, QPK * rows), jnp.bfloat16),
        ],
        compiler_params=roomy,
        cost_estimate=pl.CostEstimate(
            flops=10 * rows * keys * HD * QPK, bytes_accessed=4 * sent.size, transcendentals=rows * keys * QPK
        ),
    )(begins, first, sent)


def split_kernel(core_ref, x_ref, keep_ref, send_ref):
    core = core_ref[0]
    tokens = x_ref.shape[0]
    for group in range(16):
        y, zl = divmod(group, 4)
        turned = x_ref[:, group * 256:(group + 1) * 256].astype(jnp.float32).T.reshape(16, 16, tokens)
        lower = turned[:, :8].reshape(128, tokens)
        upper = turned[:, 8:].reshape(128, tokens)
        keep = jnp.where(core == 0, lower, upper).astype(jnp.bfloat16)
        send = jnp.where(core == 0, upper, lower).astype(jnp.bfloat16)
        for x in range(4):
            at = (y * 4 + x) * 128 + zl * 32
            keep_ref[at:at + 32, :] = keep[x * 32:(x + 1) * 32]
            send_ref[at:at + 32, :] = send[x * 32:(x + 1) * 32]


def split_features(core, inputs):
    rows, width = inputs.shape
    shape = jax.ShapeDtypeStruct((width // 2, rows), jnp.bfloat16)
    return pl.pallas_call(
        split_kernel,
        out_shape=(shape, shape),
        in_specs=[smem, vmem],
        out_specs=(vmem, vmem),
        compiler_params=roomy,
        cost_estimate=pl.CostEstimate(flops=4 * inputs.size, bytes_accessed=4 * inputs.size, transcendentals=0),
    )(core, inputs)


def pack_kernel(q_ref, g_ref, mine_ref, other_ref, sent_ref):
    sent_ref[:, :, :WIDTH] = q_ref[...].reshape(COLS, OWN, WIDTH)
    sent_ref[:, :, WIDTH:2 * WIDTH] = g_ref[...].reshape(COLS, OWN, WIDTH)
    kv = (mine_ref[...] + other_ref[...]).astype(jnp.bfloat16).reshape(COLS, OWN, 2 * HD)
    for k in range(BLOCKS):
        back = BLOCKS - 1 - k
        at = 2 * WIDTH + 2 * k * HD
        if back:
            sent_ref[:back, :, at:at + 2 * HD] = jnp.zeros((back, OWN, 2 * HD), jnp.bfloat16)
        sent_ref[back:, :, at:at + 2 * HD] = kv[:COLS - back]


def pack(queries, grads, mine, other):
    return pl.pallas_call(
        pack_kernel,
        out_shape=jax.ShapeDtypeStruct((COLS, OWN, FEATURES), jnp.bfloat16),
        in_specs=[vmem] * 4,
        out_specs=vmem,
        compiler_params=roomy,
        cost_estimate=pl.CostEstimate(flops=mine.size, bytes_accessed=8 * queries.size, transcendentals=0),
    )(queries, grads, mine, other)


def fold_kernel(back_ref, dkv_ref):
    def part(k):
        at = 2 * WIDTH + 2 * k * HD
        return back_ref[:, :, at:at + 2 * HD].astype(jnp.float32)

    total = part(BLOCKS - 1)
    for k in range(1, BLOCKS):
        fill = jnp.zeros((k, OWN, 2 * HD), jnp.float32)
        total = total + jnp.concatenate([part(BLOCKS - 1 - k)[k:], fill], axis=0)
    dkv_ref[...] = total.reshape(COLS * OWN, 2 * HD).astype(jnp.bfloat16)


def fold(back):
    return pl.pallas_call(
        fold_kernel,
        out_shape=jax.ShapeDtypeStruct((COLS * OWN, 2 * HD), jnp.bfloat16),
        in_specs=[vmem],
        out_specs=vmem,
        compiler_params=roomy,
        cost_estimate=pl.CostEstimate(flops=back.size, bytes_accessed=back.size, transcendentals=0),
    )(back)


def weight_kernel(keep_ref, recv_ref, mine_ref, other_ref, out_ref):
    for at in range(0, keep_ref.shape[0], 256):
        rows = slice(at, at + 256)
        total = lax.dot_general(keep_ref[rows], mine_ref[...], plain_dims, preferred_element_type=jnp.float32)
        total += lax.dot_general(recv_ref[rows], other_ref[...], plain_dims, preferred_element_type=jnp.float32)
        out_ref[rows] = total.astype(out_ref.dtype)


def weight_part(keep, recv, mine, other):
    return pl.pallas_call(
        weight_kernel,
        out_shape=jax.ShapeDtypeStruct((keep.shape[0], 2 * HD), jnp.bfloat16),
        in_specs=[vmem] * 4,
        out_specs=vmem,
        compiler_params=roomy,
        cost_estimate=pl.CostEstimate(flops=8 * keep.size * HD, bytes_accessed=6 * keep.size, transcendentals=0),
    )(keep, recv, mine, other)


def exchange(array, axes):
    return lax.all_to_all(array, axes, split_axis=0, concat_axis=0, tiled=True)


def spread(array, axes):
    count = lax.axis_size(axes)
    return exchange(jnp.broadcast_to(array[None], (count,) + array.shape), axes)


def swap(array):
    return lax.ppermute(array, "core", [(0, 1), (1, 0)])


def per_device(layer_input, queries, grad_out, key_weight, value_weight, doc_len):
    inputs = layer_input[0]
    core = lax.axis_index("core").astype(jnp.int32).reshape(1)
    place = lax.axis_index(CTX)
    ends = jnp.cumsum(doc_len[0])
    units = place * OWN + jnp.arange(OWN, dtype=jnp.int32)
    begins = jnp.max(jnp.where(ends[None, :] <= units[:, None], ends[None, :], 0), axis=1)
    first = (place * OWN).astype(jnp.int32).reshape(1)

    keep, send = split_features(core, inputs)
    line = spread(jnp.concatenate([key_weight, value_weight], axis=1), LINE)
    line, keep, send, begins, first = lax.optimization_barrier((line, keep, send, begins, first))
    recv = swap(send)
    weight = spread(line, PLANE).reshape(keep.shape[0], 2 * HD)

    other = lax.dot_general(recv, weight, first_dims, preferred_element_type=jnp.float32)
    other = swap(other)
    mine = lax.dot_general(keep, weight, first_dims, preferred_element_type=jnp.float32)

    sent = exchange(pack(queries[0], grad_out[0], mine, other), CTX)
    back = exchange(attention(begins, first, sent), CTX)

    dkv = fold(back)
    part = weight_part(keep, recv, dkv, swap(dkv)).reshape(16, -1, 2 * HD)
    plane = jnp.sum(exchange(part, PLANE).astype(jnp.float32), axis=0).reshape(16, -1, 2 * HD)
    share = jnp.sum(exchange(plane, LINE), axis=0)

    rows = back.reshape(COLS * OWN, FEATURES)
    return (rows[None, :, :WIDTH], rows[None, :, WIDTH:2 * WIDTH], share[:, :HD], share[:, HD:])


def solution(mesh):
    split = Mesh(mesh.devices.reshape(4, 4, 4, 4, 2), SPLIT)
    isl = ("zh", "core")
    placed = (
        P(isl, CTX, None),
        P(isl, CTX, None),
        P(isl, CTX, None),
        P(SPLIT, None),
        P(SPLIT, None),
        P(isl, None),
    )
    return jax.shard_map(
        per_device,
        mesh=split,
        in_specs=placed,
        out_specs=(
            P(isl, CTX, None),
            P(isl, CTX, None),
            P(SPLIT, None),
            P(SPLIT, None),
        ),
        check_vma=False,
    )
```

time: 254 us -> 202 us (0.80)
  local copies, waits for them, and re-layouts: 30.2 us -> 5.15 us
  waiting for transfers between devices: 47.8 us -> 23.6 us
  starting transfers between devices: 14.2 us -> 27.1 us
  other arithmetic: 10.5 us -> 1.92 us
  blocking collectives: 135 us -> 129 us
    all_to_all x2, waiting for transfers between devices: 47.8 us -> 21.2 us  [exchange(): return lax.all_to_all(array, axes, split_axis=0, concat_axis=0, tiled=True)]
    all_to_all x2, starting transfers between devices: 12.3 us -> 21.2 us  [exchange(): return lax.all_to_all(array, axes, split_axis=0, concat_axis=0, tiled=True)]
    all_to_all x3 -> x0, local copies, waits for them, and re-layouts: 7.96 us -> none  [exchange(): return lax.all_to_all(array, axes, split_axis=0, concat_axis=0, tiled=True)]
    reduce_sum x3 -> x2, other arithmetic: 7.35 us -> 0.8 us  [the longest x1 0.78 us: per_device(): jnp.sum(exchange(part, PLANE).astype(jnp.float32), axis=0)]
    all_to_all x5 -> x4, blocking collectives: 135 us -> 129 us  [exchange(): return lax.all_to_all(array, axes, split_axis=0, concat_axis=0, tiled=True)]
    dot_general x1 -> x0, local copies, waits for them, and re-layouts: 5.6 us -> none  [per_device(): lax.dot_general(inputs, dkv.astype(jnp.bfloat16), first_dims, preferred_e...]
    unnamed x10 -> x6, local copies, waits for them, and re-layouts: 6.73 us -> 1.6 us
    concatenate x8 -> x0, local copies, waits for them, and re-layouts: 4.96 us -> none  [the longest x6 4.91 us: per_device(): sent = jnp.concatenate([queries[0], grad_out[0]] + window, axis=1)]
  transfers between devices with their start and end apart: 3 -> 5, of which waited for: 2 -> 4; matrix products, arithmetic and copies ran while one was open for 4% -> 2% of each run, Pallas kernels for 0% -> 0%
where the time goes in v2:
time: 202 us; the launch traced here: 201 us
  blocking collectives  129 us (64%)
  starting transfers between devices  27.1 us (13%)
  waiting for transfers between devices  23.6 us (12%)
  Pallas kernels  12.4 us (6%)
  local copies, waits for them, and re-layouts  5.15 us (3%)
    all_to_all x4, blocking collectives, exchange(): return lax.all_to_all(array, axes, split_axis=0, concat_axis=0, tiled=True)  129 us
    all_to_all x2, waiting for transfers between devices, exchange(): return lax.all_to_all(array, axes, split_axis=0, concat_axis=0, tiled=True)  21.2 us
    all_to_all x2, starting transfers between devices, exchange(): return lax.all_to_all(array, axes, split_axis=0, concat_axis=0, tiled=True)  21.2 us
    pallas_call x1, Pallas kernels, attention(): pl.pallas_call(attention_kernel, out_shape=jax.ShapeDtypeStruct(sent.shap...  10.8 us
    ppermute x3, starting transfers between devices, swap(): return lax.ppermute(array, 'core', [(0, 1), (1, 0)])  5.88 us
  transfers between devices with their start and end apart: 5, of which 4 were waited for; matrix products, arithmetic and copies ran while one was open for 2% of the time, Pallas kernels for 0%

profile of v2, /device:TPU:32, one launch (start us, length us, event | category | flops | bytes accessed | tf_op | source)
XLA Modules:
  0.0 201.2 jit_solution(16049893816857413372)
XLA Ops:
  0.6 0.7 pad_maximum_fusion
  1.3 0.6 broadcast_in_dim.18
  2.0 15.2 %all-to-all-start = ((bf16[16,8,256]{2,1,0:T(8,128)(2,1)}), bf16[16,8,256]{2,1,0:T(8,128)(2,1)S(1)}, u32[]{:S(2)}, u32[]{:S(2)}) async-start(bf16[16,8,256]{2,1,0:T(8,128)(2,1)} %broadcast_in_dim.18), calls=%async_computation | async-start | bytes 131072 | tf_op jit(solution)/shard_map/all_to_all | solution.py:212
  17.2 0.8 copy.12
  17.9 0.1 reduce-window.8
  18.1 0.1 reduce
  18.2 0.0 copy-start
  18.2 1.6 copy-done
  19.8 0.6 shard_map.93
  20.4 0.2 select_reduce_fusion.begin_ref
  20.6 8.7 %all-to-all-done = bf16[16,8,256]{2,1,0:T(8,128)(2,1)S(1)} async-done(((bf16[16,8,256]{2,1,0:T(8,128)(2,1)}), bf16[16,8,256]{2,1,0:T(8,128)(2,1)S(1)}, u32[]{:S(2)}, u32[]{:S(2)}) %all-to-all-start) | async-done | bytes 65568 | tf_op jit(solution)/shard_map/all_to_all | solution.py:212
  29.3 1.9 collective-permute-start
  31.3 0.1 broadcast_in_dim.20
  31.4 24.7 %all_to_all.30 = bf16[16,16,8,256]{3,2,1,0:T(8,128)(2,1)S(1)} all-to-all(bf16[16,16,8,256]{3,2,1,0:T(8,128)(2,1)S(1)} %broadcast_in_dim.20), channel_id=1, replica_groups=mesh['y'=4,'zl'=4,'x'=4,'zh'=4,'core'=2] {'y','x'}, dimensions={0} | all-to-all | bytes 2097152 | tf_op jit(solution)/shard_map/all_to_all | solution.py:212
  56.1 0.0 collective-permute-done.recv_ref
  56.1 0.5 fusion.2
  56.5 0.0 copy-start.1
  56.5 0.0 copy-start.2
  56.6 2.1 %collective-permute-start.1 = (f32[256,256]{1,0:T(8,128)S(1)}, f32[256,256]{1,0:T(8,128)S(1)}, u32[]{:S(2)}, u32[]{:S(2)}) collective-permute-start(f32[256,256]{1,0:T(8,128)S(1)} %fusion.2), channel_id=1, source_target_pairs={{0,1},{1,0},{2,3},{3,2},{4,5},{5,4},{6,7},{7,6},{8,9},{9,8},{10,11... | collective-permute-start | bytes 786440 | tf_op jit(solution)/shard_map/ppermute | solution.py:221
  58.6 0.5 fusion.1.mine_ref
  59.1 1.0 collective-permute-done.1.other_ref
  60.1 0.0 copy-done.1
  60.1 0.0 copy-done.2
  60.1 0.2 shard_map.94
  60.3 39.8 %all_to_all.31.sent_ref = bf16[64,4,2816]{2,1,0:T(4,128)(2,1)S(1)} all-to-all(bf16[64,4,2816]{2,1,0:T(4,128)(2,1)S(1)} %shard_map.94), channel_id=1, replica_groups=mesh['y'=4,'zl'=4,'x'=4,'zh'=4,'core'=2] {'y','zl','x'}, dimensions={0} | all-to-all | bytes 2883584 | tf_op jit(solution)/shard_map/all_to_all | solution.py:212
  100.1 10.8 %shard_map.95 = bf16[64,4,2816]{2,1,0:T(4,128)(2,1)S(1)} custom-call(s32[4]{0:T(128)S(1)} %select_reduce_fusion.begin_ref, s32[1]{0:T(128)} %bitcast.3.first_ref, bf16[64,4,2816]{2,1,0:T(4,128)(2,1)S(1)} %all_to_all.31.sent_ref), custom_call_target="tpu_custom_call" | custom-call | flops 2013265920 | bytes 2883584 | tf_op jit(solution)/shard_map/pallas_call | solution.py:99
  110.9 42.3 %all_to_all.32.back_ref = bf16[64,4,2816]{2,1,0:T(4,128)(2,1)S(1)} all-to-all(bf16[64,4,2816]{2,1,0:T(4,128)(2,1)S(1)} %shard_map.95), channel_id=1, replica_groups=mesh['y'=4,'zl'=4,'x'=4,'zh'=4,'core'=2] {'y','zl','x'}, dimensions={0} | all-to-all | bytes 2883584 | tf_op jit(solution)/shard_map/all_to_all | solution.py:212
  153.1 0.1 shard_map.96.mine_ref
  153.2 1.9 collective-permute-start.2
  155.1 1.3 collective-permute-done.2.other_ref
  156.5 0.7 shard_map.97
  157.2 22.7 %all_to_all.33 = bf16[16,128,256]{2,1,0:T(8,128)(2,1)S(1)} all-to-all(bf16[16,128,256]{2,1,0:T(8,128)(2,1)S(1)} %bitcast.17), channel_id=1, replica_groups=mesh['y'=4,'zl'=4,'x'=4,'zh'=4,'core'=2] {'y','x'}, dimensions={0} | all-to-all | bytes 2097152 | tf_op jit(solution)/shard_map/all_to_all | solution.py:212
  179.8 0.8 convert_reduce_fusion
  180.6 6.0 %all-to-all-start.5 = ((f32[16,8,256]{2,1,0:T(8,128)}), f32[16,8,256]{2,1,0:T(8,128)S(1)}, u32[]{:S(2)}, u32[]{:S(2)}) async-start(f32[16,8,256]{2,1,0:T(8,128)} %bitcast.10), calls=%async_computation.5 | async-start | bytes 262144 | tf_op jit(solution)/shard_map/all_to_all | solution.py:212
  186.6 0.3 reshape.61
  187.0 1.1 slice_bitcast_fusion
  188.1 12.5 %all-to-all-done.5 = f32[16,8,256]{2,1,0:T(8,128)S(1)} async-done(((f32[16,8,256]{2,1,0:T(8,128)}), f32[16,8,256]{2,1,0:T(8,128)S(1)}, u32[]{:S(2)}, u32[]{:S(2)}) %all-to-all-start.5) | async-done | bytes 131104 | tf_op jit(solution)/shard_map/all_to_all | solution.py:212
  200.6 0.6 fusion
  (2 shorter events, 0.0 us)
Async XLA Ops:
  2.0 27.4 %all-to-all-start = ((bf16[16,8,256]{2,1,0:T(8,128)(2,1)}), bf16[16,8,256]{2,1,0:T(8,128)(2,1)S(1)}, u32[]{:S(2)}, u32[]{:S(2)}) async-start(bf16[16,8,256]{2,1,0:T(8,128)(2,1)} %broadcast_in_dim.18), calls=%async_computation | async-start | bytes 131072 | tf_op jit(solution)/shard_map/all_to_all | solution.py:212
  18.2 1.6 copy-start
  29.3 26.7 %collective-permute-start = (bf16[2048,256]{1,0:T(8,128)(2,1)S(1)}, bf16[2048,256]{1,0:T(8,128)(2,1)S(1)}, u32[]{:S(2)}, u32[]{:S(2)}) collective-permute-start(bf16[2048,256]{1,0:T(8,128)(2,1)S(1)} %get-tuple-element.17), channel_id=1, source_target_pairs={{0,1},{1,0},{2,3},{3,2},{4,5},{5,4},{6,7},{7,6},{8,9},{9,8},{10,11... | collective-permute-start | bytes 3145736 | tf_op jit(solution)/shard_map/ppermute | solution.py:221
  56.5 3.6 %copy-start.1 = (bf16[1,256,1024]{2,1,0:T(8,128)(2,1)S(1)}, bf16[1,256,1024]{2,1,0:T(8,128)(2,1)}, u32[]{:S(2)}) copy-start(bf16[1,256,1024]{2,1,0:T(8,128)(2,1)} %param.7) | copy-start | bytes 1572868
  56.5 3.6 %copy-start.2 = (bf16[1,256,1024]{2,1,0:T(8,128)(2,1)S(1)}, bf16[1,256,1024]{2,1,0:T(8,128)(2,1)}, u32[]{:S(2)}) copy-start(bf16[1,256,1024]{2,1,0:T(8,128)(2,1)} %param.8) | copy-start | bytes 1572868
  56.6 3.6 %collective-permute-start.1 = (f32[256,256]{1,0:T(8,128)S(1)}, f32[256,256]{1,0:T(8,128)S(1)}, u32[]{:S(2)}, u32[]{:S(2)}) collective-permute-start(f32[256,256]{1,0:T(8,128)S(1)} %fusion.2), channel_id=1, source_target_pairs={{0,1},{1,0},{2,3},{3,2},{4,5},{5,4},{6,7},{7,6},{8,9},{9,8},{10,11... | collective-permute-start | bytes 786440 | tf_op jit(solution)/shard_map/ppermute | solution.py:221
  153.2 3.2 %collective-permute-start.2 = (bf16[256,256]{1,0:T(8,128)(2,1)S(1)}, bf16[256,256]{1,0:T(8,128)(2,1)S(1)}, u32[]{:S(2)}, u32[]{:S(2)}) collective-permute-start(bf16[256,256]{1,0:T(8,128)(2,1)S(1)} %shard_map.96.mine_ref), channel_id=1, source_target_pairs={{0,1},{1,0},{2,3},{3,2},{4,5},{5,4},{6,7},{7,6},{8,9},{9,8},{10,11... | collective-permute-start | bytes 393224 | tf_op jit(solution)/shard_map/ppermute | solution.py:221
  180.6 20.0 %all-to-all-start.5 = ((f32[16,8,256]{2,1,0:T(8,128)}), f32[16,8,256]{2,1,0:T(8,128)S(1)}, u32[]{:S(2)}, u32[]{:S(2)}) async-start(f32[16,8,256]{2,1,0:T(8,128)} %bitcast.10), calls=%async_computation.5 | async-start | bytes 262144 | tf_op jit(solution)/shard_map/all_to_all | solution.py:212

commit v3 on v2

--- a/solution.py
+++ b/solution.py
@@ -28,7 +28,7 @@
 roomy = pltpu.CompilerParams(vmem_limit_bytes=40 * 1024 * 1024)
 
 
-def attention_kernel(begin_ref, first_ref, sent_ref, back_ref, got_ref, bias_ref, p_ref, ds_ref):
+def attention_kernel(begin_ref, first_ref, sent_ref, back_ref, got_ref, bias_ref, dkey_ref, dvalue_ref):
     rows = COLS * OWN
     keys = BLOCKS * rows
     first = first_ref[0]
@@ -56,41 +56,63 @@
 
     key, value = window(0), window(1)
     key_t, value_t = key.T, value.T
-    for head in range(QPK):
-        cols = slice(head * HD, (head + 1) * HD)
-        gcols = slice(WIDTH + head * HD, WIDTH + (head + 1) * HD)
-        part = slice(head * rows, (head + 1) * rows)
-        query = got_ref[:, cols]
-        grad = got_ref[:, gcols]
-        grad_t = grad.T.astype(jnp.float32)
-        score = lax.dot_general(key, query, last_dims, preferred_element_type=jnp.float32)
-        score = score * factor + bias_ref[...]
-        expo = jnp.exp2(score - jnp.max(score, axis=0, keepdims=True))
-        probs = expo * (1.0 / jnp.sum(expo, axis=0, keepdims=True))
-        low = probs.astype(jnp.bfloat16)
-        p_ref[:, part] = low
-        out_t = lax.dot_general(value_t, low, plain_dims, preferred_element_type=jnp.float32)
-        out_t = out_t.astype(jnp.bfloat16)
-        back_ref[:, :, cols] = out_t.T.reshape(COLS, OWN, HD)
-        delta = jnp.sum(grad_t * out_t.astype(jnp.float32), axis=0, keepdims=True)
-        dprobs = lax.dot_general(value, grad, last_dims, preferred_element_type=jnp.float32)
-        dscore = (probs * (dprobs - delta)).astype(jnp.bfloat16)
-        ds_ref[:, part] = dscore
-        dq_t = lax.dot_general(key_t, dscore, plain_dims, preferred_element_type=jnp.float32) * scale
-        back_ref[:, :, gcols] = dq_t.astype(jnp.bfloat16).T.reshape(COLS, OWN, HD)
+    held = {}
+
+    def query(head):
+        return got_ref[:, head * HD:(head + 1) * HD]
+
+    def grad(head):
+        return got_ref[:, WIDTH + head * HD:WIDTH + (head + 1) * HD]
+
+    def put(at, block):
+        back_ref[:, :, at:at + HD] = block.astype(jnp.bfloat16).reshape(COLS, OWN, HD)
+
+    def add(ref, head, term):
+        if head:
+            ref[...] += term
+        else:
+            ref[...] = term
+
+    def score(head):
+        held["score", head] = lax.dot_general(key, query(head), last_dims, preferred_element_type=jnp.float32)
+
+    def softmax(head):
+        scaled = held.pop(("score", head)) * factor + bias_ref[...]
+        expo = jnp.exp2(scaled - jnp.max(scaled, axis=0, keepdims=True))
+        held["probs", head] = expo * (1.0 / jnp.sum(expo, axis=0, keepdims=True))
+        held["low", head] = held["probs", head].astype(jnp.bfloat16)
+
+    def dvalues(head):
+        add(dvalue_ref, head, lax.dot_general(held.pop(("low", head)), grad(head), plain_dims, preferred_element_type=jnp.float32))
+
+    def dprobs(head):
+        held["dprobs", head] = lax.dot_general(value, grad(head), last_dims, preferred_element_type=jnp.float32)
+
+    def output(head):
+        out_t = lax.dot_general(value_t, held["low", head], plain_dims, preferred_element_type=jnp.float32).astype(jnp.bfloat16)
+        put(head * HD, out_t.T)
+        product = grad(head).T.astype(jnp.float32) * out_t.astype(jnp.float32)
+        held["delta", head] = jnp.sum(product, axis=0, keepdims=True)
+
+    def dscores(head):
+        difference = held.pop(("dprobs", head)) - held.pop(("delta", head))
+        held["dscores", head] = (held.pop(("probs", head)) * difference).astype(jnp.bfloat16)
+
+    def dqueries(head):
+        dscore = held.pop(("dscores", head))
+        dquery_t = lax.dot_general(key_t, dscore, plain_dims, preferred_element_type=jnp.float32) * scale
+        put(WIDTH + head * HD, dquery_t.astype(jnp.bfloat16).T)
+        add(dkey_ref, head, lax.dot_general(dscore, query(head), plain_dims, preferred_element_type=jnp.float32))
+
+    order = ((score, 0), (softmax, 1), (dvalues, 2), (dprobs, 1), (output, 1), (dqueries, 2), (dscores, 1))
+    for turn in range(QPK + 2):
+        for step, lag in order:
+            if 0 <= turn - lag < QPK:
+                step(turn - lag)
     for k in range(BLOCKS):
         block = slice(k * rows, (k + 1) * rows)
-        dkey = jnp.zeros((rows, HD), jnp.float32)
-        dvalue = jnp.zeros((rows, HD), jnp.float32)
-        for head in range(QPK):
-            cols = slice(head * HD, (head + 1) * HD)
-            gcols = slice(WIDTH + head * HD, WIDTH + (head + 1) * HD)
-            part = slice(head * rows, (head + 1) * rows)
-            dkey += lax.dot_general(ds_ref[block, part], got_ref[:, cols], plain_dims, preferred_element_type=jnp.float32)
-            dvalue += lax.dot_general(p_ref[block, part], got_ref[:, gcols], plain_dims, preferred_element_type=jnp.float32)
-        at = 2 * WIDTH + 2 * k * HD
-        back_ref[:, :, at:at + HD] = (dkey * scale).astype(jnp.bfloat16).reshape(COLS, OWN, HD)
-        back_ref[:, :, at + HD:at + 2 * HD] = dvalue.astype(jnp.bfloat16).reshape(COLS, OWN, HD)
+        put(2 * WIDTH + 2 * k * HD, dkey_ref[block] * scale)
+        put(2 * WIDTH + (2 * k + 1) * HD, dvalue_ref[block])
 
 
 def attention(begins, first, sent):
@@ -104,8 +126,8 @@
         scratch_shapes=[
             pltpu.VMEM((rows, FEATURES), jnp.bfloat16),
             pltpu.VMEM((keys, rows), jnp.float32),
-            pltpu.VMEM((keys, QPK * rows), jnp.bfloat16),
-            pltpu.VMEM((keys, QPK * rows), jnp.bfloat16),
+            pltpu.VMEM((keys, HD), jnp.float32),
+            pltpu.VMEM((keys, HD), jnp.float32),
         ],
         compiler_params=roomy,
         cost_estimate=pl.CostEstimate(
@@ -217,6 +239,22 @@
     return exchange(jnp.broadcast_to(array[None], (count,) + array.shape), axes)
 
 
+def copies_kernel(key_ref, value_ref, out_ref):
+    out_ref[:, :, :HD] = jnp.broadcast_to(key_ref[...][None], out_ref.shape[:2] + (HD,))
+    out_ref[:, :, HD:] = jnp.broadcast_to(value_ref[...][None], out_ref.shape[:2] + (HD,))
+
+
+def weight_copies(key_weight, value_weight, count):
+    rows = key_weight.shape[0]
+    return pl.pallas_call(
+        copies_kernel,
+        out_shape=jax.ShapeDtypeStruct((count, rows, 2 * HD), jnp.bfloat16),
+        in_specs=[vmem] * 2,
+        out_specs=vmem,
+        cost_estimate=pl.CostEstimate(flops=0, bytes_accessed=4 * count * rows * HD, transcendentals=0),
+    )(key_weight, value_weight)
+
+
 def swap(array):
     return lax.ppermute(array, "core", [(0, 1), (1, 0)])
 
@@ -231,7 +269,7 @@
     first = (place * OWN).astype(jnp.int32).reshape(1)
 
     keep, send = split_features(core, inputs)
-    line = spread(jnp.concatenate([key_weight, value_weight], axis=1), LINE)
+    line = exchange(weight_copies(key_weight, value_weight, 16), LINE)
     line, keep, send, begins, first = lax.optimization_barrier((line, keep, send, begins, first))
     recv = swap(send)
     weight = spread(line, PLANE).reshape(keep.shape[0], 2 * HD)

time: 202 us -> 197 us (0.975)
  Pallas kernels: 12.4 us -> 9.38 us
    pallas_call x1, Pallas kernels: 10.8 us -> 6.5 us  [attention(): pl.pallas_call(attention_kernel, out_shape=jax.ShapeDtypeStruct(sent.shap...]
where the time goes in v3:
time: 197 us
  blocking collectives  129 us (65%)
  starting transfers between devices  27.1 us (14%)
  waiting for transfers between devices  23.6 us (12%)
  Pallas kernels  9.38 us (5%)
  local copies, waits for them, and re-layouts  4.51 us (2%)
    all_to_all x4, blocking collectives, exchange(): return lax.all_to_all(array, axes, split_axis=0, concat_axis=0, tiled=True)  129 us
    all_to_all x2, waiting for transfers between devices, exchange(): return lax.all_to_all(array, axes, split_axis=0, concat_axis=0, tiled=True)  21.2 us
    all_to_all x2, starting transfers between devices, exchange(): return lax.all_to_all(array, axes, split_axis=0, concat_axis=0, tiled=True)  21.2 us
    pallas_call x1, Pallas kernels, attention(): pl.pallas_call(attention_kernel, out_shape=jax.ShapeDtypeStruct(sent.shap...  6.5 us
    ppermute x3, starting transfers between devices, swap(): return lax.ppermute(array, 'core', [(0, 1), (1, 0)])  5.88 us
  transfers between devices with their start and end apart: 5, of which 4 were waited for; matrix products, arithmetic and copies ran while one was open for 2% of the time, Pallas kernels for 0%

profile of v3, /device:TPU:32, one launch (start us, length us, event | category | flops | bytes accessed | tf_op | source)
XLA Modules:
  0.0 196.9 jit_solution(4714424535793210023)
XLA Ops:
  0.6 1.3 shard_map.93
  2.0 15.2 %all-to-all-start = ((bf16[16,8,256]{2,1,0:T(8,128)(2,1)}), bf16[16,8,256]{2,1,0:T(8,128)(2,1)S(1)}, u32[]{:S(2)}, u32[]{:S(2)}) async-start(bf16[16,8,256]{2,1,0:T(8,128)(2,1)} %shard_map.93), calls=%async_computation | async-start | bytes 131072 | tf_op jit(solution)/shard_map/all_to_all | solution.py:234
  17.2 0.8 copy.12
  17.9 0.1 reduce-window.8
  18.1 0.1 reduce
  18.2 0.0 copy-start
  18.2 1.6 copy-done
  19.8 0.6 shard_map.94
  20.4 0.2 select_reduce_fusion.begin_ref
  20.6 8.7 %all-to-all-done = bf16[16,8,256]{2,1,0:T(8,128)(2,1)S(1)} async-done(((bf16[16,8,256]{2,1,0:T(8,128)(2,1)}), bf16[16,8,256]{2,1,0:T(8,128)(2,1)S(1)}, u32[]{:S(2)}, u32[]{:S(2)}) %all-to-all-start) | async-done | bytes 65568 | tf_op jit(solution)/shard_map/all_to_all | solution.py:234
  29.3 1.9 collective-permute-start
  31.3 0.1 broadcast_in_dim.26
  31.4 24.7 %all_to_all.30 = bf16[16,16,8,256]{3,2,1,0:T(8,128)(2,1)S(1)} all-to-all(bf16[16,16,8,256]{3,2,1,0:T(8,128)(2,1)S(1)} %broadcast_in_dim.26), channel_id=1, replica_groups=mesh['y'=4,'zl'=4,'x'=4,'zh'=4,'core'=2] {'y','x'}, dimensions={0} | all-to-all | bytes 2097152 | tf_op jit(solution)/shard_map/all_to_all | solution.py:234
  56.1 0.0 collective-permute-done.recv_ref
  56.1 0.5 fusion.2
  56.5 0.0 copy-start.1
  56.5 0.0 copy-start.2
  56.6 2.1 %collective-permute-start.1 = (f32[256,256]{1,0:T(8,128)S(1)}, f32[256,256]{1,0:T(8,128)S(1)}, u32[]{:S(2)}, u32[]{:S(2)}) collective-permute-start(f32[256,256]{1,0:T(8,128)S(1)} %fusion.2), channel_id=1, source_target_pairs={{0,1},{1,0},{2,3},{3,2},{4,5},{5,4},{6,7},{7,6},{8,9},{9,8},{10,11... | collective-permute-start | bytes 786440 | tf_op jit(solution)/shard_map/ppermute | solution.py:259
  58.6 0.5 fusion.1.mine_ref
  59.1 1.0 collective-permute-done.1.other_ref
  60.1 0.0 copy-done.1
  60.1 0.0 copy-done.2
  60.1 0.2 shard_map.95
  60.3 39.8 %all_to_all.31.sent_ref = bf16[64,4,2816]{2,1,0:T(4,128)(2,1)S(1)} all-to-all(bf16[64,4,2816]{2,1,0:T(4,128)(2,1)S(1)} %shard_map.95), channel_id=1, replica_groups=mesh['y'=4,'zl'=4,'x'=4,'zh'=4,'core'=2] {'y','zl','x'}, dimensions={0} | all-to-all | bytes 2883584 | tf_op jit(solution)/shard_map/all_to_all | solution.py:234
  100.1 6.5 %shard_map.96 = bf16[64,4,2816]{2,1,0:T(4,128)(2,1)S(1)} custom-call(s32[4]{0:T(128)S(1)} %select_reduce_fusion.begin_ref, s32[1]{0:T(128)} %bitcast.3.first_ref, bf16[64,4,2816]{2,1,0:T(4,128)(2,1)S(1)} %all_to_all.31.sent_ref), custom_call_target="tpu_custom_call" | custom-call | flops 2013265920 | bytes 2883584 | tf_op jit(solution)/shard_map/pallas_call | solution.py:121
  106.6 42.3 %all_to_all.32.back_ref = bf16[64,4,2816]{2,1,0:T(4,128)(2,1)S(1)} all-to-all(bf16[64,4,2816]{2,1,0:T(4,128)(2,1)S(1)} %shard_map.96), channel_id=1, replica_groups=mesh['y'=4,'zl'=4,'x'=4,'zh'=4,'core'=2] {'y','zl','x'}, dimensions={0} | all-to-all | bytes 2883584 | tf_op jit(solution)/shard_map/all_to_all | solution.py:234
  148.8 0.1 shard_map.97.mine_ref
  148.9 1.9 collective-permute-start.2
  150.8 1.3 collective-permute-done.2.other_ref
  152.2 0.7 shard_map.98
  152.9 22.7 %all_to_all.33 = bf16[16,128,256]{2,1,0:T(8,128)(2,1)S(1)} all-to-all(bf16[16,128,256]{2,1,0:T(8,128)(2,1)S(1)} %bitcast.17), channel_id=1, replica_groups=mesh['y'=4,'zl'=4,'x'=4,'zh'=4,'core'=2] {'y','x'}, dimensions={0} | all-to-all | bytes 2097152 | tf_op jit(solution)/shard_map/all_to_all | solution.py:234
  175.5 0.8 convert_reduce_fusion
  176.3 6.0 %all-to-all-start.5 = ((f32[16,8,256]{2,1,0:T(8,128)}), f32[16,8,256]{2,1,0:T(8,128)S(1)}, u32[]{:S(2)}, u32[]{:S(2)}) async-start(f32[16,8,256]{2,1,0:T(8,128)} %bitcast.10), calls=%async_computation.5 | async-start | bytes 262144 | tf_op jit(solution)/shard_map/all_to_all | solution.py:234
  182.3 0.3 reshape.60
  182.7 1.1 slice_bitcast_fusion
  183.8 12.5 %all-to-all-done.5 = f32[16,8,256]{2,1,0:T(8,128)S(1)} async-done(((f32[16,8,256]{2,1,0:T(8,128)}), f32[16,8,256]{2,1,0:T(8,128)S(1)}, u32[]{:S(2)}, u32[]{:S(2)}) %all-to-all-start.5) | async-done | bytes 131104 | tf_op jit(solution)/shard_map/all_to_all | solution.py:234
  196.3 0.6 fusion
  (2 shorter events, 0.0 us)
Async XLA Ops:
  2.0 27.4 %all-to-all-start = ((bf16[16,8,256]{2,1,0:T(8,128)(2,1)}), bf16[16,8,256]{2,1,0:T(8,128)(2,1)S(1)}, u32[]{:S(2)}, u32[]{:S(2)}) async-start(bf16[16,8,256]{2,1,0:T(8,128)(2,1)} %shard_map.93), calls=%async_computation | async-start | bytes 131072 | tf_op jit(solution)/shard_map/all_to_all | solution.py:234
  18.2 1.6 copy-start
  29.3 26.7 %collective-permute-start = (bf16[2048,256]{1,0:T(8,128)(2,1)S(1)}, bf16[2048,256]{1,0:T(8,128)(2,1)S(1)}, u32[]{:S(2)}, u32[]{:S(2)}) collective-permute-start(bf16[2048,256]{1,0:T(8,128)(2,1)S(1)} %get-tuple-element.17), channel_id=1, source_target_pairs={{0,1},{1,0},{2,3},{3,2},{4,5},{5,4},{6,7},{7,6},{8,9},{9,8},{10,11... | collective-permute-start | bytes 3145736 | tf_op jit(solution)/shard_map/ppermute | solution.py:259
  56.5 3.6 %copy-start.1 = (bf16[1,256,1024]{2,1,0:T(8,128)(2,1)S(1)}, bf16[1,256,1024]{2,1,0:T(8,128)(2,1)}, u32[]{:S(2)}) copy-start(bf16[1,256,1024]{2,1,0:T(8,128)(2,1)} %param.7) | copy-start | bytes 1572868
  56.5 3.6 %copy-start.2 = (bf16[1,256,1024]{2,1,0:T(8,128)(2,1)S(1)}, bf16[1,256,1024]{2,1,0:T(8,128)(2,1)}, u32[]{:S(2)}) copy-start(bf16[1,256,1024]{2,1,0:T(8,128)(2,1)} %param.8) | copy-start | bytes 1572868
  56.6 3.6 %collective-permute-start.1 = (f32[256,256]{1,0:T(8,128)S(1)}, f32[256,256]{1,0:T(8,128)S(1)}, u32[]{:S(2)}, u32[]{:S(2)}) collective-permute-start(f32[256,256]{1,0:T(8,128)S(1)} %fusion.2), channel_id=1, source_target_pairs={{0,1},{1,0},{2,3},{3,2},{4,5},{5,4},{6,7},{7,6},{8,9},{9,8},{10,11... | collective-permute-start | bytes 786440 | tf_op jit(solution)/shard_map/ppermute | solution.py:259
  148.9 3.2 %collective-permute-start.2 = (bf16[256,256]{1,0:T(8,128)(2,1)S(1)}, bf16[256,256]{1,0:T(8,128)(2,1)S(1)}, u32[]{:S(2)}, u32[]{:S(2)}) collective-permute-start(bf16[256,256]{1,0:T(8,128)(2,1)S(1)} %shard_map.97.mine_ref), channel_id=1, source_target_pairs={{0,1},{1,0},{2,3},{3,2},{4,5},{5,4},{6,7},{7,6},{8,9},{9,8},{10,11... | collective-permute-start | bytes 393224 | tf_op jit(solution)/shard_map/ppermute | solution.py:259
  176.3 20.0 %all-to-all-start.5 = ((f32[16,8,256]{2,1,0:T(8,128)}), f32[16,8,256]{2,1,0:T(8,128)S(1)}, u32[]{:S(2)}, u32[]{:S(2)}) async-start(f32[16,8,256]{2,1,0:T(8,128)} %bitcast.10), calls=%async_computation.5 | async-start | bytes 262144 | tf_op jit(solution)/shard_map/all_to_all | solution.py:234

commit v4 on v3

--- a/solution.py
+++ b/solution.py
@@ -16,7 +16,8 @@
 
 SPLIT = ("y", "zl", "x", "zh", "core")
 CTX = ("y", "zl", "x")
-PLANE = ("y", "x")
+PEERS = ("zl", "x", "y")
+PLANE = ("x", "y")
 LINE = ("zl", "zh")
 last_dims = (((1,), (1,)), ((), ()))
 plain_dims = (((1,), (0,)), ((), ()))
@@ -28,6 +29,10 @@
 roomy = pltpu.CompilerParams(vmem_limit_bytes=40 * 1024 * 1024)
 
 
+def column_of(peer):
+    return (peer % 4) * 16 + (peer // 16) * 4 + peer // 4 % 4
+
+
 def attention_kernel(begin_ref, first_ref, sent_ref, back_ref, got_ref, bias_ref, dkey_ref, dvalue_ref):
     rows = COLS * OWN
     keys = BLOCKS * rows
@@ -38,12 +43,12 @@
 
     key_row = lax.broadcasted_iota(jnp.int32, (keys, 1), 0)
     key_block = key_row // rows
-    key_col = (key_row - key_block * rows) // OWN
+    key_col = column_of((key_row - key_block * rows) // OWN)
     key_unit = first + (key_block - (BLOCKS - 1)) * OWN + key_row % OWN
     key_pos = key_unit * COLS + key_col
     row = lax.broadcasted_iota(jnp.int32, (1, rows), 1)
     slot = row % OWN
-    row_pos = (first + slot) * COLS + row // OWN
+    row_pos = (first + slot) * COLS + column_of(row // OWN)
     start = jnp.zeros((1, rows), jnp.int32)
     for i in range(OWN):
         start = jnp.where(slot == i, begin_ref[i], start)
@@ -147,7 +152,7 @@
         keep = jnp.where(core == 0, lower, upper).astype(jnp.bfloat16)
         send = jnp.where(core == 0, upper, lower).astype(jnp.bfloat16)
         for x in range(4):
-            at = (y * 4 + x) * 128 + zl * 32
+            at = (x * 4 + y) * 128 + zl * 32
             keep_ref[at:at + 32, :] = keep[x * 32:(x + 1) * 32]
             send_ref[at:at + 32, :] = send[x * 32:(x + 1) * 32]
 
@@ -211,25 +216,6 @@
     )(back)
 
 
-def weight_kernel(keep_ref, recv_ref, mine_ref, other_ref, out_ref):
-    for at in range(0, keep_ref.shape[0], 256):
-        rows = slice(at, at + 256)
-        total = lax.dot_general(keep_ref[rows], mine_ref[...], plain_dims, preferred_element_type=jnp.float32)
-        total += lax.dot_general(recv_ref[rows], other_ref[...], plain_dims, preferred_element_type=jnp.float32)
-        out_ref[rows] = total.astype(out_ref.dtype)
-
-
-def weight_part(keep, recv, mine, other):
-    return pl.pallas_call(
-        weight_kernel,
-        out_shape=jax.ShapeDtypeStruct((keep.shape[0], 2 * HD), jnp.bfloat16),
-        in_specs=[vmem] * 4,
-        out_specs=vmem,
-        compiler_params=roomy,
-        cost_estimate=pl.CostEstimate(flops=8 * keep.size * HD, bytes_accessed=6 * keep.size, transcendentals=0),
-    )(keep, recv, mine, other)
-
-
 def exchange(array, axes):
     return lax.all_to_all(array, axes, split_axis=0, concat_axis=0, tiled=True)
 
@@ -239,22 +225,6 @@
     return exchange(jnp.broadcast_to(array[None], (count,) + array.shape), axes)
 
 
-def copies_kernel(key_ref, value_ref, out_ref):
-    out_ref[:, :, :HD] = jnp.broadcast_to(key_ref[...][None], out_ref.shape[:2] + (HD,))
-    out_ref[:, :, HD:] = jnp.broadcast_to(value_ref[...][None], out_ref.shape[:2] + (HD,))
-
-
-def weight_copies(key_weight, value_weight, count):
-    rows = key_weight.shape[0]
-    return pl.pallas_call(
-        copies_kernel,
-        out_shape=jax.ShapeDtypeStruct((count, rows, 2 * HD), jnp.bfloat16),
-        in_specs=[vmem] * 2,
-        out_specs=vmem,
-        cost_estimate=pl.CostEstimate(flops=0, bytes_accessed=4 * count * rows * HD, transcendentals=0),
-    )(key_weight, value_weight)
-
-
 def swap(array):
     return lax.ppermute(array, "core", [(0, 1), (1, 0)])
 
@@ -262,27 +232,27 @@
 def per_device(layer_input, queries, grad_out, key_weight, value_weight, doc_len):
     inputs = layer_input[0]
     core = lax.axis_index("core").astype(jnp.int32).reshape(1)
-    place = lax.axis_index(CTX)
+    place = lax.axis_index(PEERS)
     ends = jnp.cumsum(doc_len[0])
     units = place * OWN + jnp.arange(OWN, dtype=jnp.int32)
     begins = jnp.max(jnp.where(ends[None, :] <= units[:, None], ends[None, :], 0), axis=1)
     first = (place * OWN).astype(jnp.int32).reshape(1)
 
+    line = spread(jnp.concatenate([key_weight, value_weight], axis=1), LINE)
     keep, send = split_features(core, inputs)
-    line = exchange(weight_copies(key_weight, value_weight, 16), LINE)
     line, keep, send, begins, first = lax.optimization_barrier((line, keep, send, begins, first))
-    recv = swap(send)
     weight = spread(line, PLANE).reshape(keep.shape[0], 2 * HD)
 
-    other = lax.dot_general(recv, weight, first_dims, preferred_element_type=jnp.float32)
-    other = swap(other)
+    other = lax.dot_general(send, swap(weight), first_dims, preferred_element_type=jnp.float32)
     mine = lax.dot_general(keep, weight, first_dims, preferred_element_type=jnp.float32)
 
-    sent = exchange(pack(queries[0], grad_out[0], mine, other), CTX)
-    back = exchange(attention(begins, first, sent), CTX)
+    sent = exchange(pack(queries[0], grad_out[0], mine, other), PEERS)
+    back = exchange(attention(begins, first, sent), PEERS)
 
     dkv = fold(back)
-    part = weight_part(keep, recv, dkv, swap(dkv)).reshape(16, -1, 2 * HD)
+    away = jnp.dot(send, dkv, preferred_element_type=jnp.float32).astype(jnp.bfloat16)
+    part = jnp.dot(keep, dkv, preferred_element_type=jnp.float32) + swap(away).astype(jnp.float32)
+    part = part.astype(jnp.bfloat16).reshape(16, -1, 2 * HD)
     plane = jnp.sum(exchange(part, PLANE).astype(jnp.float32), axis=0).reshape(16, -1, 2 * HD)
     share = jnp.sum(exchange(plane, LINE), axis=0)
 

time: 197 us -> 195 us (0.990)
  starting transfers between devices: 27.1 us -> 25 us
  blocking collectives: 129 us -> 127 us
    all_to_all x4, blocking collectives: 129 us -> 127 us  [exchange(): return lax.all_to_all(array, axes, split_axis=0, concat_axis=0, tiled=True)]
    ppermute x3 -> x2, waiting for transfers between devices: 2.34 us -> 4.77 us  [swap(): return lax.ppermute(array, 'core', [(0, 1), (1, 0)])]
    pallas_call x2 -> x0, Pallas kernels: 2.04 us -> none  [the longest x1 1.34 us: weight_copies(): pl.pallas_call(copies_kernel, out_shape=jax.ShapeDtypeStruct((count, rows...]
    ppermute x3 -> x2, starting transfers between devices: 5.88 us -> 3.96 us  [swap(): return lax.ppermute(array, 'core', [(0, 1), (1, 0)])]
  transfers between devices with their start and end apart: 5 -> 4, of which waited for: 4 -> 4; matrix products, arithmetic and copies ran while one was open for 2% -> 2% of each run, Pallas kernels for 0% -> 0%
where the time goes in v4:
time: 195 us
  blocking collectives  127 us (65%)
  waiting for transfers between devices  25.5 us (13%)
  starting transfers between devices  25 us (13%)
  Pallas kernels  7.98 us (4%)
  local copies, waits for them, and re-layouts  5.14 us (3%)
    all_to_all x4, blocking collectives, exchange(): return lax.all_to_all(array, axes, split_axis=0, concat_axis=0, tiled=True)  127 us
    all_to_all x2, starting transfers between devices, exchange(): return lax.all_to_all(array, axes, split_axis=0, concat_axis=0, tiled=True)  21 us
    all_to_all x2, waiting for transfers between devices, exchange(): return lax.all_to_all(array, axes, split_axis=0, concat_axis=0, tiled=True)  20.8 us
    pallas_call x1, Pallas kernels, attention(): pl.pallas_call(attention_kernel, out_shape=jax.ShapeDtypeStruct(sent.shap...  7.13 us
    ppermute x2, waiting for transfers between devices, swap(): return lax.ppermute(array, 'core', [(0, 1), (1, 0)])  4.77 us
    ppermute x2, starting transfers between devices, swap(): return lax.ppermute(array, 'core', [(0, 1), (1, 0)])  3.96 us
  transfers between devices with their start and end apart: 4, of which 4 were waited for; matrix products, arithmetic and copies ran while one was open for 2% of the time, Pallas kernels for 0%

profile of v4, /device:TPU:32, one launch (start us, length us, event | category | flops | bytes accessed | tf_op | source)
XLA Modules:
  0.0 194.8 jit_solution(12866781226070664675)
XLA Ops:
  0.6 0.7 pad_maximum_fusion
  1.3 0.6 broadcast_in_dim.18
  2.0 15.2 %all-to-all-start = ((bf16[16,8,256]{2,1,0:T(8,128)(2,1)}), bf16[16,8,256]{2,1,0:T(8,128)(2,1)S(1)}, u32[]{:S(2)}, u32[]{:S(2)}) async-start(bf16[16,8,256]{2,1,0:T(8,128)(2,1)} %broadcast_in_dim.18), calls=%async_computation | async-start | bytes 131072 | tf_op jit(solution)/shard_map/all_to_all | solution.py:220
  17.2 0.8 copy.12
  17.9 0.1 reduce-window.8
  18.1 0.1 reduce
  18.2 0.0 copy-start
  18.2 1.6 copy-done
  19.8 0.6 shard_map.93
  20.4 0.2 select_reduce_fusion.begin_ref
  20.6 8.7 %all-to-all-done = bf16[16,8,256]{2,1,0:T(8,128)(2,1)S(1)} async-done(((bf16[16,8,256]{2,1,0:T(8,128)(2,1)}), bf16[16,8,256]{2,1,0:T(8,128)(2,1)S(1)}, u32[]{:S(2)}, u32[]{:S(2)}) %all-to-all-start) | async-done | bytes 65568 | tf_op jit(solution)/shard_map/all_to_all | solution.py:220
  29.3 0.1 broadcast_in_dim.20
  29.4 22.6 %all_to_all.30 = bf16[16,16,8,256]{3,2,1,0:T(8,128)(2,1)S(1)} all-to-all(bf16[16,16,8,256]{3,2,1,0:T(8,128)(2,1)S(1)} %broadcast_in_dim.20), channel_id=1, replica_groups=mesh['y'=4,'zl'=4,'x'=4,'zh'=4,'core'=2] {'x','y'}, dimensions={0} | all-to-all | bytes 2097152 | tf_op jit(solution)/shard_map/all_to_all | solution.py:220
  52.0 0.0 copy-start.1
  52.0 0.0 copy-start.2
  52.0 2.0 %collective-permute-start = (bf16[2048,256]{1,0:T(8,128)(2,1)S(1)}, bf16[2048,256]{1,0:T(8,128)(2,1)S(1)}, u32[]{:S(2)}, u32[]{:S(2)}) collective-permute-start(bf16[2048,256]{1,0:T(8,128)(2,1)S(1)} %bitcast.25), channel_id=1, source_target_pairs={{0,1},{1,0},{2,3},{3,2},{4,5},{5,4},{6,7},{7,6},{8,9},{9,8},{10,11... | collective-permute-start | bytes 3145736 | tf_op jit(solution)/shard_map/ppermute | solution.py:229
  54.1 0.5 fusion.1.mine_ref
  54.6 2.1 %collective-permute-done = bf16[2048,256]{1,0:T(8,128)(2,1)S(1)} collective-permute-done((bf16[2048,256]{1,0:T(8,128)(2,1)S(1)}, bf16[2048,256]{1,0:T(8,128)(2,1)S(1)}, u32[]{:S(2)}, u32[]{:S(2)}) %collective-permute-start) | collective-permute-done | bytes 1048608 | tf_op jit(solution)/shard_map/ppermute | solution.py:229
  56.7 0.5 fusion.2.other_ref
  57.2 0.0 copy-done.1
  57.2 0.0 copy-done.2
  57.2 0.2 shard_map.94
  57.4 39.0 %all_to_all.31.sent_ref = bf16[64,4,2816]{2,1,0:T(4,128)(2,1)S(1)} all-to-all(bf16[64,4,2816]{2,1,0:T(4,128)(2,1)S(1)} %shard_map.94), channel_id=1, replica_groups=mesh['y'=4,'zl'=4,'x'=4,'zh'=4,'core'=2] {'zl','x','y'}, dimensions={0} | all-to-all | bytes 2883584 | tf_op jit(solution)/shard_map/all_to_all | solution.py:220
  96.3 7.1 %shard_map.95 = bf16[64,4,2816]{2,1,0:T(4,128)(2,1)S(1)} custom-call(s32[4]{0:T(128)S(1)} %select_reduce_fusion.begin_ref, s32[1]{0:T(128)} %bitcast.3.first_ref, bf16[64,4,2816]{2,1,0:T(4,128)(2,1)S(1)} %all_to_all.31.sent_ref), custom_call_target="tpu_custom_call" | custom-call | flops 2013265920 | bytes 2883584 | tf_op jit(solution)/shard_map/pallas_call | solution.py:126
  103.5 41.7 %all_to_all.32.back_ref = bf16[64,4,2816]{2,1,0:T(4,128)(2,1)S(1)} all-to-all(bf16[64,4,2816]{2,1,0:T(4,128)(2,1)S(1)} %shard_map.95), channel_id=1, replica_groups=mesh['y'=4,'zl'=4,'x'=4,'zh'=4,'core'=2] {'zl','x','y'}, dimensions={0} | all-to-all | bytes 2883584 | tf_op jit(solution)/shard_map/all_to_all | solution.py:220
  145.2 0.1 shard_map.96
  145.3 0.4 convolution_convert_fusion
  145.7 1.9 collective-permute-start.1
  147.6 2.6 %collective-permute-done.1 = bf16[2048,256]{1,0:T(8,128)(2,1)S(1)} collective-permute-done((bf16[2048,256]{1,0:T(8,128)(2,1)S(1)}, bf16[2048,256]{1,0:T(8,128)(2,1)S(1)}, u32[]{:S(2)}, u32[]{:S(2)}) %collective-permute-start.1) | collective-permute-done | bytes 1048608 | tf_op jit(solution)/shard_map/ppermute | solution.py:229
  150.3 0.4 add_convert_fusion
  150.7 23.4 %all_to_all.33 = bf16[16,128,256]{2,1,0:T(8,128)(2,1)S(1)} all-to-all(bf16[16,128,256]{2,1,0:T(8,128)(2,1)S(1)} %bitcast.24), channel_id=1, replica_groups=mesh['y'=4,'zl'=4,'x'=4,'zh'=4,'core'=2] {'x','y'}, dimensions={0} | all-to-all | bytes 2097152 | tf_op jit(solution)/shard_map/all_to_all | solution.py:220
  174.1 0.8 convert_reduce_fusion
  174.9 5.8 %all-to-all-start.5 = ((f32[16,8,256]{2,1,0:T(8,128)}), f32[16,8,256]{2,1,0:T(8,128)S(1)}, u32[]{:S(2)}, u32[]{:S(2)}) async-start(f32[16,8,256]{2,1,0:T(8,128)} %bitcast.10), calls=%async_computation.5 | async-start | bytes 262144 | tf_op jit(solution)/shard_map/all_to_all | solution.py:220
  180.7 0.3 reshape.61
  181.1 1.1 slice_bitcast_fusion
  182.2 12.0 %all-to-all-done.5 = f32[16,8,256]{2,1,0:T(8,128)S(1)} async-done(((f32[16,8,256]{2,1,0:T(8,128)}), f32[16,8,256]{2,1,0:T(8,128)S(1)}, u32[]{:S(2)}, u32[]{:S(2)}) %all-to-all-start.5) | async-done | bytes 131104 | tf_op jit(solution)/shard_map/all_to_all | solution.py:220
  194.2 0.6 fusion
  (2 shorter events, 0.0 us)
Async XLA Ops:
  2.0 27.4 %all-to-all-start = ((bf16[16,8,256]{2,1,0:T(8,128)(2,1)}), bf16[16,8,256]{2,1,0:T(8,128)(2,1)S(1)}, u32[]{:S(2)}, u32[]{:S(2)}) async-start(bf16[16,8,256]{2,1,0:T(8,128)(2,1)} %broadcast_in_dim.18), calls=%async_computation | async-start | bytes 131072 | tf_op jit(solution)/shard_map/all_to_all | solution.py:220
  18.2 1.6 copy-start
  52.0 5.2 %copy-start.1 = (bf16[1,256,1024]{2,1,0:T(8,128)(2,1)S(1)}, bf16[1,256,1024]{2,1,0:T(8,128)(2,1)}, u32[]{:S(2)}) copy-start(bf16[1,256,1024]{2,1,0:T(8,128)(2,1)} %param.7) | copy-start | bytes 1572868
  52.0 5.2 %copy-start.2 = (bf16[1,256,1024]{2,1,0:T(8,128)(2,1)S(1)}, bf16[1,256,1024]{2,1,0:T(8,128)(2,1)}, u32[]{:S(2)}) copy-start(bf16[1,256,1024]{2,1,0:T(8,128)(2,1)} %param.8) | copy-start | bytes 1572868
  52.0 4.7 %collective-permute-start = (bf16[2048,256]{1,0:T(8,128)(2,1)S(1)}, bf16[2048,256]{1,0:T(8,128)(2,1)S(1)}, u32[]{:S(2)}, u32[]{:S(2)}) collective-permute-start(bf16[2048,256]{1,0:T(8,128)(2,1)S(1)} %bitcast.25), channel_id=1, source_target_pairs={{0,1},{1,0},{2,3},{3,2},{4,5},{5,4},{6,7},{7,6},{8,9},{9,8},{10,11... | collective-permute-start | bytes 3145736 | tf_op jit(solution)/shard_map/ppermute | solution.py:229
  145.7 4.6 %collective-permute-start.1 = (bf16[2048,256]{1,0:T(8,128)(2,1)S(1)}, bf16[2048,256]{1,0:T(8,128)(2,1)S(1)}, u32[]{:S(2)}, u32[]{:S(2)}) collective-permute-start(bf16[2048,256]{1,0:T(8,128)(2,1)S(1)} %convolution_convert_fusion), channel_id=1, source_target_pairs={{0,1},{1,0},{2,3},{3,2},{4,5},{5,4},{6,7},{7,6},{8,9},{9,8},{10,11... | collective-permute-start | bytes 3145736 | tf_op jit(solution)/shard_map/ppermute | solution.py:229
  174.9 19.3 %all-to-all-start.5 = ((f32[16,8,256]{2,1,0:T(8,128)}), f32[16,8,256]{2,1,0:T(8,128)S(1)}, u32[]{:S(2)}, u32[]{:S(2)}) async-start(f32[16,8,256]{2,1,0:T(8,128)} %bitcast.10), calls=%async_computation.5 | async-start | bytes 262144 | tf_op jit(solution)/shard_map/all_to_all | solution.py:220

commit v5 on v4

--- a/solution.py
+++ b/solution.py
@@ -29,10 +29,6 @@
 roomy = pltpu.CompilerParams(vmem_limit_bytes=40 * 1024 * 1024)
 
 
-def column_of(peer):
-    return (peer % 4) * 16 + (peer // 16) * 4 + peer // 4 % 4
-
-
 def attention_kernel(begin_ref, first_ref, sent_ref, back_ref, got_ref, bias_ref, dkey_ref, dvalue_ref):
     rows = COLS * OWN
     keys = BLOCKS * rows
@@ -41,19 +37,20 @@
     scale = float(HD) ** -0.5
     factor = scale * math.log2(math.e)
 
-    key_row = lax.broadcasted_iota(jnp.int32, (keys, 1), 0)
-    key_block = key_row // rows
-    key_col = column_of((key_row - key_block * rows) // OWN)
-    key_unit = first + (key_block - (BLOCKS - 1)) * OWN + key_row % OWN
-    key_pos = key_unit * COLS + key_col
+    def position(row):
+        return ((row & 3) << 6) + (((row >> 2) & 3) << 4) + ((row >> 6) << 2) + ((row >> 4) & 3)
+
     row = lax.broadcasted_iota(jnp.int32, (1, rows), 1)
-    slot = row % OWN
-    row_pos = (first + slot) * COLS + column_of(row // OWN)
     start = jnp.zeros((1, rows), jnp.int32)
     for i in range(OWN):
-        start = jnp.where(slot == i, begin_ref[i], start)
-    allowed = (key_unit >= start) & (key_pos <= row_pos)
-    bias_ref[...] = jnp.where(allowed, 0.0, hidden).astype(jnp.float32)
+        start = jnp.where((row & 3) == i, (begin_ref[i] - first) * COLS, start)
+    key_pos = position(lax.broadcasted_iota(jnp.int32, (rows, 1), 0))
+    for k in range(BLOCKS):
+        shifted = key_pos - (BLOCKS - 1 - k) * OWN * COLS
+        allowed = shifted >= start
+        if k == BLOCKS - 1:
+            allowed = allowed & (shifted <= position(row))
+        bias_ref[k * rows:(k + 1) * rows] = jnp.where(allowed, 0.0, hidden).astype(jnp.float32)
 
     def window(place):
         parts = [got_ref[:, 2 * WIDTH + (2 * k + place) * HD:][:, :HD] for k in range(BLOCKS)]
@@ -232,26 +229,31 @@
 def per_device(layer_input, queries, grad_out, key_weight, value_weight, doc_len):
     inputs = layer_input[0]
     core = lax.axis_index("core").astype(jnp.int32).reshape(1)
-    place = lax.axis_index(PEERS)
-    ends = jnp.cumsum(doc_len[0])
-    units = place * OWN + jnp.arange(OWN, dtype=jnp.int32)
-    begins = jnp.max(jnp.where(ends[None, :] <= units[:, None], ends[None, :], 0), axis=1)
-    first = (place * OWN).astype(jnp.int32).reshape(1)
 
     line = spread(jnp.concatenate([key_weight, value_weight], axis=1), LINE)
     keep, send = split_features(core, inputs)
-    line, keep, send, begins, first = lax.optimization_barrier((line, keep, send, begins, first))
+    line, keep, send = lax.optimization_barrier((line, keep, send))
+    recv = swap(send)
     weight = spread(line, PLANE).reshape(keep.shape[0], 2 * HD)
 
-    other = lax.dot_general(send, swap(weight), first_dims, preferred_element_type=jnp.float32)
+    other = lax.dot_general(recv, weight, first_dims, preferred_element_type=jnp.float32)
+    other, keep, lengths = lax.optimization_barrier((other, keep, doc_len[0]))
+    other = swap(other)
     mine = lax.dot_general(keep, weight, first_dims, preferred_element_type=jnp.float32)
+
+    first = lax.axis_index(PEERS).astype(jnp.int32) * OWN
+    units = first + jnp.arange(OWN, dtype=jnp.int32)
+    numbers = jnp.arange(lengths.shape[0], dtype=jnp.int32)
+    ends = jnp.sum(jnp.where(numbers[None, :] <= numbers[:, None], lengths[None, :], 0), axis=1)
+    begins = jnp.max(jnp.where(ends[None, :] <= units[:, None], ends[None, :], 0), axis=1)
+    first = first.reshape(1)
 
     sent = exchange(pack(queries[0], grad_out[0], mine, other), PEERS)
     back = exchange(attention(begins, first, sent), PEERS)
 
     dkv = fold(back)
-    away = jnp.dot(send, dkv, preferred_element_type=jnp.float32).astype(jnp.bfloat16)
-    part = jnp.dot(keep, dkv, preferred_element_type=jnp.float32) + swap(away).astype(jnp.float32)
+    part = jnp.dot(keep, dkv, preferred_element_type=jnp.float32)
+    part = part + jnp.dot(recv, swap(dkv), preferred_element_type=jnp.float32)
     part = part.astype(jnp.bfloat16).reshape(16, -1, 2 * HD)
     plane = jnp.sum(exchange(part, PLANE).astype(jnp.float32), axis=0).reshape(16, -1, 2 * HD)
     share = jnp.sum(exchange(plane, LINE), axis=0)

time: 195 us -> 197 us (1.010)
  blocking collectives: 127 us -> 89.8 us
  waiting for transfers between devices: 25.5 us -> 56.9 us
  starting transfers between devices: 25 us -> 32.7 us
    all_to_all x4 -> x3, blocking collectives: 127 us -> 89.8 us  [exchange(): return lax.all_to_all(array, axes, split_axis=0, concat_axis=0, tiled=True)]
    all_to_all x2 -> x3, waiting for transfers between devices: 20.8 us -> 55 us  [exchange(): return lax.all_to_all(array, axes, split_axis=0, concat_axis=0, tiled=True)]
    all_to_all x2 -> x3, starting transfers between devices: 21 us -> 26.9 us  [exchange(): return lax.all_to_all(array, axes, split_axis=0, concat_axis=0, tiled=True)]
    ppermute x2 -> x3, waiting for transfers between devices: 4.77 us -> 1.92 us  [swap(): return lax.ppermute(array, 'core', [(0, 1), (1, 0)])]
    ppermute x2 -> x3, starting transfers between devices: 3.96 us -> 5.75 us  [swap(): return lax.ppermute(array, 'core', [(0, 1), (1, 0)])]
  transfers between devices with their start and end apart: 4 -> 6, of which waited for: 4 -> 5; matrix products, arithmetic and copies ran while one was open for 2% -> 1% of each run, Pallas kernels for 0% -> 0%
where the time goes in v5:
time: 197 us; the launch traced here: 196 us
  blocking collectives  89.8 us (46%)
  waiting for transfers between devices  56.9 us (29%)
  starting transfers between devices  32.7 us (17%)
  Pallas kernels  8.12 us (4%)
  local copies, waits for them, and re-layouts  4.38 us (2%)
    all_to_all x3, blocking collectives, exchange(): return lax.all_to_all(array, axes, split_axis=0, concat_axis=0, tiled=True)  89.8 us
    all_to_all x3, waiting for transfers between devices, exchange(): return lax.all_to_all(array, axes, split_axis=0, concat_axis=0, tiled=True)  55 us
    all_to_all x3, starting transfers between devices, exchange(): return lax.all_to_all(array, axes, split_axis=0, concat_axis=0, tiled=True)  26.9 us
    pallas_call x1, Pallas kernels, attention(): pl.pallas_call(attention_kernel, out_shape=jax.ShapeDtypeStruct(sent.shap...  6.15 us
    ppermute x3, starting transfers between devices, swap(): return lax.ppermute(array, 'core', [(0, 1), (1, 0)])  5.75 us
  transfers between devices with their start and end apart: 6, of which 5 were waited for; matrix products, arithmetic and copies ran while one was open for 1% of the time, Pallas kernels for 0%

profile of v5, /device:TPU:32, one launch (start us, length us, event | category | flops | bytes accessed | tf_op | source)
XLA Modules:
  0.0 196.2 jit_solution(956509964840192094)
XLA Ops:
  0.6 0.7 pad_maximum_fusion
  1.3 0.6 broadcast_in_dim.30
  2.0 15.2 %all-to-all-start = ((bf16[16,8,256]{2,1,0:T(8,128)(2,1)}), bf16[16,8,256]{2,1,0:T(8,128)(2,1)S(1)}, u32[]{:S(2)}, u32[]{:S(2)}) async-start(bf16[16,8,256]{2,1,0:T(8,128)(2,1)} %broadcast_in_dim.30), calls=%async_computation | async-start | bytes 131072 | tf_op jit(solution)/shard_map/all_to_all | solution.py:217
  17.2 0.0 copy-start
  17.2 1.6 copy-done
  18.8 0.6 shard_map.93
  19.4 9.9 %all-to-all-done = bf16[16,8,256]{2,1,0:T(8,128)(2,1)S(1)} async-done(((bf16[16,8,256]{2,1,0:T(8,128)(2,1)}), bf16[16,8,256]{2,1,0:T(8,128)(2,1)S(1)}, u32[]{:S(2)}, u32[]{:S(2)}) %all-to-all-start) | async-done | bytes 65568 | tf_op jit(solution)/shard_map/all_to_all | solution.py:217
  29.3 1.9 collective-permute-start
  31.3 0.1 broadcast_in_dim.31
  31.4 24.6 %all_to_all.30 = bf16[16,16,8,256]{3,2,1,0:T(8,128)(2,1)S(1)} all-to-all(bf16[16,16,8,256]{3,2,1,0:T(8,128)(2,1)S(1)} %broadcast_in_dim.31), channel_id=1, replica_groups=mesh['y'=4,'zl'=4,'x'=4,'zh'=4,'core'=2] {'x','y'}, dimensions={0} | all-to-all | bytes 2097152 | tf_op jit(solution)/shard_map/all_to_all | solution.py:217
  56.0 0.0 collective-permute-done
  56.0 0.0 copy-start.1
  56.0 0.0 copy-start.2
  56.0 0.5 fusion.2
  56.5 1.9 collective-permute-start.1
  58.4 0.5 fusion.3.mine_ref
  58.9 1.0 collective-permute-done.1.other_ref
  59.9 0.0 copy-done.1
  59.9 0.0 copy-done.2
  59.9 1.3 shard_map.94
  61.2 0.0 copy-start.3
  61.2 5.8 %all-to-all-start.2 = ((bf16[64,4,2816]{2,1,0:T(4,128)(2,1)}), bf16[64,4,2816]{2,1,0:T(4,128)(2,1)S(1)}, u32[]{:S(2)}, u32[]{:S(2)}) async-start(bf16[64,4,2816]{2,1,0:T(4,128)(2,1)} %shard_map.94), calls=%async_computation.2 | async-start | bytes 2883584 | tf_op jit(solution)/shard_map/all_to_all | solution.py:217
  67.0 0.0 copy-done.3
  67.0 0.1 select_reduce_fusion
  67.1 0.2 select_reduce_fusion.1.begin_ref
  67.3 33.0 %all-to-all-done.2.sent_ref = bf16[64,4,2816]{2,1,0:T(4,128)(2,1)S(1)} async-done(((bf16[64,4,2816]{2,1,0:T(4,128)(2,1)}), bf16[64,4,2816]{2,1,0:T(4,128)(2,1)S(1)}, u32[]{:S(2)}, u32[]{:S(2)}) %all-to-all-start.2) | async-done | bytes 1441824 | tf_op jit(solution)/shard_map/all_to_all | solution.py:217
  100.3 6.1 %shard_map.95 = bf16[64,4,2816]{2,1,0:T(4,128)(2,1)S(1)} custom-call(s32[4]{0:T(128)S(1)} %select_reduce_fusion.1.begin_ref, s32[1]{0:T(128)} %bitcast.4.first_ref, bf16[64,4,2816]{2,1,0:T(4,128)(2,1)S(1)} %all-to-all-done.2.sent_ref), custom_call_target="tpu_custom_call" | custom-call | flops 2013265920 | bytes 2883584 | tf_op jit(solution)/shard_map/pallas_call | solution.py:123
  106.5 41.7 %all_to_all.31.back_ref = bf16[64,4,2816]{2,1,0:T(4,128)(2,1)S(1)} all-to-all(bf16[64,4,2816]{2,1,0:T(4,128)(2,1)S(1)} %shard_map.95), channel_id=1, replica_groups=mesh['y'=4,'zl'=4,'x'=4,'zh'=4,'core'=2] {'zl','x','y'}, dimensions={0} | all-to-all | bytes 2883584 | tf_op jit(solution)/shard_map/all_to_all | solution.py:217
  148.2 0.1 shard_map.96
  148.3 1.9 collective-permute-start.2
  150.2 0.4 fusion.4
  150.6 0.9 collective-permute-done.2
  151.5 0.4 fusion
  151.9 23.4 %all_to_all.32 = bf16[16,128,256]{2,1,0:T(8,128)(2,1)S(1)} all-to-all(bf16[16,128,256]{2,1,0:T(8,128)(2,1)S(1)} %bitcast.26), channel_id=1, replica_groups=mesh['y'=4,'zl'=4,'x'=4,'zh'=4,'core'=2] {'x','y'}, dimensions={0} | all-to-all | bytes 2097152 | tf_op jit(solution)/shard_map/all_to_all | solution.py:217
  175.4 0.8 convert_reduce_fusion
  176.2 5.9 %all-to-all-start.5 = ((f32[16,8,256]{2,1,0:T(8,128)}), f32[16,8,256]{2,1,0:T(8,128)S(1)}, u32[]{:S(2)}, u32[]{:S(2)}) async-start(f32[16,8,256]{2,1,0:T(8,128)} %bitcast.10), calls=%async_computation.5 | async-start | bytes 262144 | tf_op jit(solution)/shard_map/all_to_all | solution.py:217
  182.1 0.3 reshape.37
  182.5 1.1 slice_bitcast_fusion
  183.6 12.0 %all-to-all-done.5 = f32[16,8,256]{2,1,0:T(8,128)S(1)} async-done(((f32[16,8,256]{2,1,0:T(8,128)}), f32[16,8,256]{2,1,0:T(8,128)S(1)}, u32[]{:S(2)}, u32[]{:S(2)}) %all-to-all-start.5) | async-done | bytes 131104 | tf_op jit(solution)/shard_map/all_to_all | solution.py:217
  195.6 0.6 fusion.1
  (2 shorter events, 0.0 us)
Async XLA Ops:
  2.0 27.4 %all-to-all-start = ((bf16[16,8,256]{2,1,0:T(8,128)(2,1)}), bf16[16,8,256]{2,1,0:T(8,128)(2,1)S(1)}, u32[]{:S(2)}, u32[]{:S(2)}) async-start(bf16[16,8,256]{2,1,0:T(8,128)(2,1)} %broadcast_in_dim.30), calls=%async_computation | async-start | bytes 131072 | tf_op jit(solution)/shard_map/all_to_all | solution.py:217
  17.2 1.6 copy-start
  29.3 26.6 %collective-permute-start = (bf16[2048,256]{1,0:T(8,128)(2,1)S(1)}, bf16[2048,256]{1,0:T(8,128)(2,1)S(1)}, u32[]{:S(2)}, u32[]{:S(2)}) collective-permute-start(bf16[2048,256]{1,0:T(8,128)(2,1)S(1)} %get-tuple-element.14), channel_id=1, source_target_pairs={{0,1},{1,0},{2,3},{3,2},{4,5},{5,4},{6,7},{7,6},{8,9},{9,8},{10,11... | collective-permute-start | bytes 3145736 | tf_op jit(solution)/shard_map/ppermute | solution.py:226
  56.0 3.9 %copy-start.1 = (bf16[1,256,1024]{2,1,0:T(8,128)(2,1)S(1)}, bf16[1,256,1024]{2,1,0:T(8,128)(2,1)}, u32[]{:S(2)}) copy-start(bf16[1,256,1024]{2,1,0:T(8,128)(2,1)} %param.7) | copy-start | bytes 1572868
  56.0 3.9 %copy-start.2 = (bf16[1,256,1024]{2,1,0:T(8,128)(2,1)S(1)}, bf16[1,256,1024]{2,1,0:T(8,128)(2,1)}, u32[]{:S(2)}) copy-start(bf16[1,256,1024]{2,1,0:T(8,128)(2,1)} %param.8) | copy-start | bytes 1572868
  56.5 3.4 %collective-permute-start.1 = (f32[256,256]{1,0:T(8,128)S(1)}, f32[256,256]{1,0:T(8,128)S(1)}, u32[]{:S(2)}, u32[]{:S(2)}) collective-permute-start(f32[256,256]{1,0:T(8,128)S(1)} %fusion.2), channel_id=1, source_target_pairs={{0,1},{1,0},{2,3},{3,2},{4,5},{5,4},{6,7},{7,6},{8,9},{9,8},{10,11... | collective-permute-start | bytes 786440 | tf_op jit(solution)/shard_map/ppermute | solution.py:226
  61.2 5.8 %copy-start.3 = (s32[1,85]{1,0:T(1,128)S(1)}, s32[1,85]{1,0:T(1,128)}, u32[]{:S(2)}) copy-start(s32[1,85]{1,0:T(1,128)} %param.11) | copy-start | bytes 1024
  61.2 39.1 %all-to-all-start.2 = ((bf16[64,4,2816]{2,1,0:T(4,128)(2,1)}), bf16[64,4,2816]{2,1,0:T(4,128)(2,1)S(1)}, u32[]{:S(2)}, u32[]{:S(2)}) async-start(bf16[64,4,2816]{2,1,0:T(4,128)(2,1)} %shard_map.94), calls=%async_computation.2 | async-start | bytes 2883584 | tf_op jit(solution)/shard_map/all_to_all | solution.py:217
  148.3 3.2 %collective-permute-start.2 = (bf16[256,256]{1,0:T(8,128)(2,1)S(1)}, bf16[256,256]{1,0:T(8,128)(2,1)S(1)}, u32[]{:S(2)}, u32[]{:S(2)}) collective-permute-start(bf16[256,256]{1,0:T(8,128)(2,1)S(1)} %shard_map.96), channel_id=1, source_target_pairs={{0,1},{1,0},{2,3},{3,2},{4,5},{5,4},{6,7},{7,6},{8,9},{9,8},{10,11... | collective-permute-start | bytes 393224 | tf_op jit(solution)/shard_map/ppermute | solution.py:226
  176.2 19.4 %all-to-all-start.5 = ((f32[16,8,256]{2,1,0:T(8,128)}), f32[16,8,256]{2,1,0:T(8,128)S(1)}, u32[]{:S(2)}, u32[]{:S(2)}) async-start(f32[16,8,256]{2,1,0:T(8,128)} %bitcast.10), calls=%async_computation.5 | async-start | bytes 262144 | tf_op jit(solution)/shard_map/all_to_all | solution.py:217

commit v6 on v5

--- a/solution.py
+++ b/solution.py
@@ -233,12 +233,11 @@
     line = spread(jnp.concatenate([key_weight, value_weight], axis=1), LINE)
     keep, send = split_features(core, inputs)
     line, keep, send = lax.optimization_barrier((line, keep, send))
-    recv = swap(send)
     weight = spread(line, PLANE).reshape(keep.shape[0], 2 * HD)
 
-    other = lax.dot_general(recv, weight, first_dims, preferred_element_type=jnp.float32)
-    other, keep, lengths = lax.optimization_barrier((other, keep, doc_len[0]))
-    other = swap(other)
+    weight, lengths = lax.optimization_barrier((weight, doc_len[0]))
+
+    other = lax.dot_general(send, swap(weight), first_dims, preferred_element_type=jnp.float32)
     mine = lax.dot_general(keep, weight, first_dims, preferred_element_type=jnp.float32)
 
     first = lax.axis_index(PEERS).astype(jnp.int32) * OWN
@@ -252,8 +251,8 @@
     back = exchange(attention(begins, first, sent), PEERS)
 
     dkv = fold(back)
-    part = jnp.dot(keep, dkv, preferred_element_type=jnp.float32)
-    part = part + jnp.dot(recv, swap(dkv), preferred_element_type=jnp.float32)
+    away = jnp.dot(send, dkv, preferred_element_type=jnp.float32).astype(jnp.bfloat16)
+    part = jnp.dot(keep, dkv, preferred_element_type=jnp.float32) + swap(away).astype(jnp.float32)
     part = part.astype(jnp.bfloat16).reshape(16, -1, 2 * HD)
     plane = jnp.sum(exchange(part, PLANE).astype(jnp.float32), axis=0).reshape(16, -1, 2 * HD)
     share = jnp.sum(exchange(plane, LINE), axis=0)

time: 197 us -> 196 us (level)
  waiting for transfers between devices: 56.9 us -> 59.7 us
  blocking collectives: 89.8 us -> 87.7 us
    ppermute x3 -> x2, waiting for transfers between devices: 1.92 us -> 4.78 us  [swap(): return lax.ppermute(array, 'core', [(0, 1), (1, 0)])]
    all_to_all x3, blocking collectives: 89.8 us -> 87.7 us  [exchange(): return lax.all_to_all(array, axes, split_axis=0, concat_axis=0, tiled=True)]
    ppermute x3 -> x2, starting transfers between devices: 5.75 us -> 3.96 us  [swap(): return lax.ppermute(array, 'core', [(0, 1), (1, 0)])]
  transfers between devices with their start and end apart: 6 -> 5, of which waited for: 5 -> 5; matrix products, arithmetic and copies ran while one was open for 1% -> 1% of each run, Pallas kernels for 0% -> 0%
where the time goes in v6:
time: 196 us; the launch traced here: 195 us
  blocking collectives  87.7 us (45%)
  waiting for transfers between devices  59.7 us (30%)
  starting transfers between devices  31 us (16%)
  Pallas kernels  8.12 us (4%)
  local copies, waits for them, and re-layouts  4.38 us (2%)
    all_to_all x3, blocking collectives, exchange(): return lax.all_to_all(array, axes, split_axis=0, concat_axis=0, tiled=True)  87.7 us
    all_to_all x3, waiting for transfers between devices, exchange(): return lax.all_to_all(array, axes, split_axis=0, concat_axis=0, tiled=True)  54.9 us
    all_to_all x3, starting transfers between devices, exchange(): return lax.all_to_all(array, axes, split_axis=0, concat_axis=0, tiled=True)  27 us
    pallas_call x1, Pallas kernels, attention(): pl.pallas_call(attention_kernel, out_shape=jax.ShapeDtypeStruct(sent.shap...  6.15 us
    ppermute x2, waiting for transfers between devices, swap(): return lax.ppermute(array, 'core', [(0, 1), (1, 0)])  4.78 us
    ppermute x2, starting transfers between devices, swap(): return lax.ppermute(array, 'core', [(0, 1), (1, 0)])  3.96 us
  transfers between devices with their start and end apart: 5, of which 5 were waited for; matrix products, arithmetic and copies ran while one was open for 1% of the time, Pallas kernels for 0%

profile of v6, /device:TPU:32, one launch (start us, length us, event | category | flops | bytes accessed | tf_op | source)
XLA Modules:
  0.0 195.3 jit_solution(17546570600319658082)
XLA Ops:
  0.6 0.7 pad_maximum_fusion
  1.3 0.6 broadcast_in_dim.30
  2.0 15.2 %all-to-all-start = ((bf16[16,8,256]{2,1,0:T(8,128)(2,1)}), bf16[16,8,256]{2,1,0:T(8,128)(2,1)S(1)}, u32[]{:S(2)}, u32[]{:S(2)}) async-start(bf16[16,8,256]{2,1,0:T(8,128)(2,1)} %broadcast_in_dim.30), calls=%async_computation | async-start | bytes 131072 | tf_op jit(solution)/shard_map/all_to_all | solution.py:217
  17.2 0.0 copy-start
  17.2 1.6 copy-done
  18.8 0.6 shard_map.93
  19.4 9.9 %all-to-all-done = bf16[16,8,256]{2,1,0:T(8,128)(2,1)S(1)} async-done(((bf16[16,8,256]{2,1,0:T(8,128)(2,1)}), bf16[16,8,256]{2,1,0:T(8,128)(2,1)S(1)}, u32[]{:S(2)}, u32[]{:S(2)}) %all-to-all-start) | async-done | bytes 65568 | tf_op jit(solution)/shard_map/all_to_all | solution.py:217
  29.3 0.1 broadcast_in_dim.31
  29.4 22.6 %all_to_all.30 = bf16[16,16,8,256]{3,2,1,0:T(8,128)(2,1)S(1)} all-to-all(bf16[16,16,8,256]{3,2,1,0:T(8,128)(2,1)S(1)} %broadcast_in_dim.31), channel_id=1, replica_groups=mesh['y'=4,'zl'=4,'x'=4,'zh'=4,'core'=2] {'x','y'}, dimensions={0} | all-to-all | bytes 2097152 | tf_op jit(solution)/shard_map/all_to_all | solution.py:217
  52.0 0.0 copy-start.1
  52.0 0.0 copy-start.2
  52.0 2.0 %collective-permute-start = (bf16[2048,256]{1,0:T(8,128)(2,1)S(1)}, bf16[2048,256]{1,0:T(8,128)(2,1)S(1)}, u32[]{:S(2)}, u32[]{:S(2)}) collective-permute-start(bf16[2048,256]{1,0:T(8,128)(2,1)S(1)} %bitcast.25), channel_id=1, source_target_pairs={{0,1},{1,0},{2,3},{3,2},{4,5},{5,4},{6,7},{7,6},{8,9},{9,8},{10,11... | collective-permute-start | bytes 3145736 | tf_op jit(solution)/shard_map/ppermute | solution.py:226
  54.1 0.5 fusion.1.mine_ref
  54.6 2.2 %collective-permute-done = bf16[2048,256]{1,0:T(8,128)(2,1)S(1)} collective-permute-done((bf16[2048,256]{1,0:T(8,128)(2,1)S(1)}, bf16[2048,256]{1,0:T(8,128)(2,1)S(1)}, u32[]{:S(2)}, u32[]{:S(2)}) %collective-permute-start) | collective-permute-done | bytes 1048608 | tf_op jit(solution)/shard_map/ppermute | solution.py:226
  56.7 0.5 fusion.2.other_ref
  57.2 0.0 copy-done.1
  57.2 0.0 copy-done.2
  57.2 1.3 shard_map.94
  58.5 0.0 copy-start.3
  58.5 6.0 %all-to-all-start.2 = ((bf16[64,4,2816]{2,1,0:T(4,128)(2,1)}), bf16[64,4,2816]{2,1,0:T(4,128)(2,1)S(1)}, u32[]{:S(2)}, u32[]{:S(2)}) async-start(bf16[64,4,2816]{2,1,0:T(4,128)(2,1)} %shard_map.94), calls=%async_computation.2 | async-start | bytes 2883584 | tf_op jit(solution)/shard_map/all_to_all | solution.py:217
  64.5 0.0 copy-done.3
  64.5 0.1 select_reduce_fusion
  64.6 0.2 select_reduce_fusion.1.begin_ref
  64.8 33.0 %all-to-all-done.2.sent_ref = bf16[64,4,2816]{2,1,0:T(4,128)(2,1)S(1)} async-done(((bf16[64,4,2816]{2,1,0:T(4,128)(2,1)}), bf16[64,4,2816]{2,1,0:T(4,128)(2,1)S(1)}, u32[]{:S(2)}, u32[]{:S(2)}) %all-to-all-start.2) | async-done | bytes 1441824 | tf_op jit(solution)/shard_map/all_to_all | solution.py:217
  97.8 6.1 %shard_map.95 = bf16[64,4,2816]{2,1,0:T(4,128)(2,1)S(1)} custom-call(s32[4]{0:T(128)S(1)} %select_reduce_fusion.1.begin_ref, s32[1]{0:T(128)} %bitcast.4.first_ref, bf16[64,4,2816]{2,1,0:T(4,128)(2,1)S(1)} %all-to-all-done.2.sent_ref), custom_call_target="tpu_custom_call" | custom-call | flops 2013265920 | bytes 2883584 | tf_op jit(solution)/shard_map/pallas_call | solution.py:123
  104.0 41.7 %all_to_all.31.back_ref = bf16[64,4,2816]{2,1,0:T(4,128)(2,1)S(1)} all-to-all(bf16[64,4,2816]{2,1,0:T(4,128)(2,1)S(1)} %shard_map.95), channel_id=1, replica_groups=mesh['y'=4,'zl'=4,'x'=4,'zh'=4,'core'=2] {'zl','x','y'}, dimensions={0} | all-to-all | bytes 2883584 | tf_op jit(solution)/shard_map/all_to_all | solution.py:217
  145.7 0.1 shard_map.96
  145.8 0.4 convolution_convert_fusion
  146.2 1.9 collective-permute-start.1
  148.1 2.6 %collective-permute-done.1 = bf16[2048,256]{1,0:T(8,128)(2,1)S(1)} collective-permute-done((bf16[2048,256]{1,0:T(8,128)(2,1)S(1)}, bf16[2048,256]{1,0:T(8,128)(2,1)S(1)}, u32[]{:S(2)}, u32[]{:S(2)}) %collective-permute-start.1) | collective-permute-done | bytes 1048608 | tf_op jit(solution)/shard_map/ppermute | solution.py:226
  150.7 0.4 add_convert_fusion
  151.2 23.4 %all_to_all.32 = bf16[16,128,256]{2,1,0:T(8,128)(2,1)S(1)} all-to-all(bf16[16,128,256]{2,1,0:T(8,128)(2,1)S(1)} %bitcast.24), channel_id=1, replica_groups=mesh['y'=4,'zl'=4,'x'=4,'zh'=4,'core'=2] {'x','y'}, dimensions={0} | all-to-all | bytes 2097152 | tf_op jit(solution)/shard_map/all_to_all | solution.py:217
  174.6 0.8 convert_reduce_fusion
  175.4 5.8 %all-to-all-start.5 = ((f32[16,8,256]{2,1,0:T(8,128)}), f32[16,8,256]{2,1,0:T(8,128)S(1)}, u32[]{:S(2)}, u32[]{:S(2)}) async-start(f32[16,8,256]{2,1,0:T(8,128)} %bitcast.10), calls=%async_computation.5 | async-start | bytes 262144 | tf_op jit(solution)/shard_map/all_to_all | solution.py:217
  181.2 0.3 reshape.37
  181.6 1.1 slice_bitcast_fusion
  182.7 12.0 %all-to-all-done.5 = f32[16,8,256]{2,1,0:T(8,128)S(1)} async-done(((f32[16,8,256]{2,1,0:T(8,128)}), f32[16,8,256]{2,1,0:T(8,128)S(1)}, u32[]{:S(2)}, u32[]{:S(2)}) %all-to-all-start.5) | async-done | bytes 131104 | tf_op jit(solution)/shard_map/all_to_all | solution.py:217
  194.7 0.6 fusion
  (2 shorter events, 0.0 us)
Async XLA Ops:
  2.0 27.4 %all-to-all-start = ((bf16[16,8,256]{2,1,0:T(8,128)(2,1)}), bf16[16,8,256]{2,1,0:T(8,128)(2,1)S(1)}, u32[]{:S(2)}, u32[]{:S(2)}) async-start(bf16[16,8,256]{2,1,0:T(8,128)(2,1)} %broadcast_in_dim.30), calls=%async_computation | async-start | bytes 131072 | tf_op jit(solution)/shard_map/all_to_all | solution.py:217
  17.2 1.6 copy-start
  52.0 5.2 %copy-start.1 = (bf16[1,256,1024]{2,1,0:T(8,128)(2,1)S(1)}, bf16[1,256,1024]{2,1,0:T(8,128)(2,1)}, u32[]{:S(2)}) copy-start(bf16[1,256,1024]{2,1,0:T(8,128)(2,1)} %param.7) | copy-start | bytes 1572868
  52.0 5.2 %copy-start.2 = (bf16[1,256,1024]{2,1,0:T(8,128)(2,1)S(1)}, bf16[1,256,1024]{2,1,0:T(8,128)(2,1)}, u32[]{:S(2)}) copy-start(bf16[1,256,1024]{2,1,0:T(8,128)(2,1)} %param.8) | copy-start | bytes 1572868
  52.0 4.7 %collective-permute-start = (bf16[2048,256]{1,0:T(8,128)(2,1)S(1)}, bf16[2048,256]{1,0:T(8,128)(2,1)S(1)}, u32[]{:S(2)}, u32[]{:S(2)}) collective-permute-start(bf16[2048,256]{1,0:T(8,128)(2,1)S(1)} %bitcast.25), channel_id=1, source_target_pairs={{0,1},{1,0},{2,3},{3,2},{4,5},{5,4},{6,7},{7,6},{8,9},{9,8},{10,11... | collective-permute-start | bytes 3145736 | tf_op jit(solution)/shard_map/ppermute | solution.py:226
  58.5 6.0 %copy-start.3 = (s32[1,85]{1,0:T(1,128)S(1)}, s32[1,85]{1,0:T(1,128)}, u32[]{:S(2)}) copy-start(s32[1,85]{1,0:T(1,128)} %param.11) | copy-start | bytes 1024
  58.5 39.3 %all-to-all-start.2 = ((bf16[64,4,2816]{2,1,0:T(4,128)(2,1)}), bf16[64,4,2816]{2,1,0:T(4,128)(2,1)S(1)}, u32[]{:S(2)}, u32[]{:S(2)}) async-start(bf16[64,4,2816]{2,1,0:T(4,128)(2,1)} %shard_map.94), calls=%async_computation.2 | async-start | bytes 2883584 | tf_op jit(solution)/shard_map/all_to_all | solution.py:217
  146.2 4.6 %collective-permute-start.1 = (bf16[2048,256]{1,0:T(8,128)(2,1)S(1)}, bf16[2048,256]{1,0:T(8,128)(2,1)S(1)}, u32[]{:S(2)}, u32[]{:S(2)}) collective-permute-start(bf16[2048,256]{1,0:T(8,128)(2,1)S(1)} %convolution_convert_fusion), channel_id=1, source_target_pairs={{0,1},{1,0},{2,3},{3,2},{4,5},{5,4},{6,7},{7,6},{8,9},{9,8},{10,11... | collective-permute-start | bytes 3145736 | tf_op jit(solution)/shard_map/ppermute | solution.py:226
  175.4 19.3 %all-to-all-start.5 = ((f32[16,8,256]{2,1,0:T(8,128)}), f32[16,8,256]{2,1,0:T(8,128)S(1)}, u32[]{:S(2)}, u32[]{:S(2)}) async-start(f32[16,8,256]{2,1,0:T(8,128)} %bitcast.10), calls=%async_computation.5 | async-start | bytes 262144 | tf_op jit(solution)/shard_map/all_to_all | solution.py:217

commit v7 on v6

--- a/solution.py
+++ b/solution.py
@@ -229,23 +229,19 @@
 def per_device(layer_input, queries, grad_out, key_weight, value_weight, doc_len):
     inputs = layer_input[0]
     core = lax.axis_index("core").astype(jnp.int32).reshape(1)
+    place = lax.axis_index(PEERS)
+    ends = jnp.cumsum(doc_len[0])
+    units = place * OWN + jnp.arange(OWN, dtype=jnp.int32)
+    begins = jnp.max(jnp.where(ends[None, :] <= units[:, None], ends[None, :], 0), axis=1)
+    first = (place * OWN).astype(jnp.int32).reshape(1)
 
     line = spread(jnp.concatenate([key_weight, value_weight], axis=1), LINE)
     keep, send = split_features(core, inputs)
-    line, keep, send = lax.optimization_barrier((line, keep, send))
+    line, keep, send, begins, first = lax.optimization_barrier((line, keep, send, begins, first))
     weight = spread(line, PLANE).reshape(keep.shape[0], 2 * HD)
-
-    weight, lengths = lax.optimization_barrier((weight, doc_len[0]))
 
     other = lax.dot_general(send, swap(weight), first_dims, preferred_element_type=jnp.float32)
     mine = lax.dot_general(keep, weight, first_dims, preferred_element_type=jnp.float32)
-
-    first = lax.axis_index(PEERS).astype(jnp.int32) * OWN
-    units = first + jnp.arange(OWN, dtype=jnp.int32)
-    numbers = jnp.arange(lengths.shape[0], dtype=jnp.int32)
-    ends = jnp.sum(jnp.where(numbers[None, :] <= numbers[:, None], lengths[None, :], 0), axis=1)
-    begins = jnp.max(jnp.where(ends[None, :] <= units[:, None], ends[None, :], 0), axis=1)
-    first = first.reshape(1)
 
     sent = exchange(pack(queries[0], grad_out[0], mine, other), PEERS)
     back = exchange(attention(begins, first, sent), PEERS)

time: 196 us -> 194 us (0.990)
  blocking collectives: 87.7 us -> 127 us
  waiting for transfers between devices: 59.7 us -> 25.5 us
  starting transfers between devices: 31 us -> 25 us
    all_to_all x3 -> x4, blocking collectives: 87.7 us -> 127 us  [exchange(): return lax.all_to_all(array, axes, split_axis=0, concat_axis=0, tiled=True)]
    all_to_all x3 -> x2, waiting for transfers between devices: 54.9 us -> 20.8 us  [exchange(): return lax.all_to_all(array, axes, split_axis=0, concat_axis=0, tiled=True)]
    all_to_all x3 -> x2, starting transfers between devices: 27 us -> 21 us  [exchange(): return lax.all_to_all(array, axes, split_axis=0, concat_axis=0, tiled=True)]
  transfers between devices with their start and end apart: 5 -> 4, of which waited for: 5 -> 4; matrix products, arithmetic and copies ran while one was open for 1% -> 2% of each run, Pallas kernels for 0% -> 0%
where the time goes in v7:
time: 194 us
  blocking collectives  127 us (65%)
  waiting for transfers between devices  25.5 us (13%)
  starting transfers between devices  25 us (13%)
  Pallas kernels  7.05 us (4%)
  local copies, waits for them, and re-layouts  5.14 us (3%)
    all_to_all x4, blocking collectives, exchange(): return lax.all_to_all(array, axes, split_axis=0, concat_axis=0, tiled=True)  127 us
    all_to_all x2, starting transfers between devices, exchange(): return lax.all_to_all(array, axes, split_axis=0, concat_axis=0, tiled=True)  21 us
    all_to_all x2, waiting for transfers between devices, exchange(): return lax.all_to_all(array, axes, split_axis=0, concat_axis=0, tiled=True)  20.8 us
    pallas_call x1, Pallas kernels, attention(): pl.pallas_call(attention_kernel, out_shape=jax.ShapeDtypeStruct(sent.shap...  6.2 us
    ppermute x2, waiting for transfers between devices, swap(): return lax.ppermute(array, 'core', [(0, 1), (1, 0)])  4.77 us
    ppermute x2, starting transfers between devices, swap(): return lax.ppermute(array, 'core', [(0, 1), (1, 0)])  3.96 us
  transfers between devices with their start and end apart: 4, of which 4 were waited for; matrix products, arithmetic and copies ran while one was open for 2% of the time, Pallas kernels for 0%

profile of v7, /device:TPU:32, one launch (start us, length us, event | category | flops | bytes accessed | tf_op | source)
XLA Modules:
  0.0 193.9 jit_solution(3207032892249592044)
XLA Ops:
  0.6 0.7 pad_maximum_fusion
  1.3 0.6 broadcast_in_dim.18
  2.0 15.2 %all-to-all-start = ((bf16[16,8,256]{2,1,0:T(8,128)(2,1)}), bf16[16,8,256]{2,1,0:T(8,128)(2,1)S(1)}, u32[]{:S(2)}, u32[]{:S(2)}) async-start(bf16[16,8,256]{2,1,0:T(8,128)(2,1)} %broadcast_in_dim.18), calls=%async_computation | async-start | bytes 131072 | tf_op jit(solution)/shard_map/all_to_all | solution.py:217
  17.2 0.8 copy.12
  17.9 0.1 reduce-window.8
  18.1 0.1 reduce
  18.2 0.0 copy-start
  18.2 1.6 copy-done
  19.8 0.6 shard_map.93
  20.4 0.2 select_reduce_fusion.begin_ref
  20.6 8.7 %all-to-all-done = bf16[16,8,256]{2,1,0:T(8,128)(2,1)S(1)} async-done(((bf16[16,8,256]{2,1,0:T(8,128)(2,1)}), bf16[16,8,256]{2,1,0:T(8,128)(2,1)S(1)}, u32[]{:S(2)}, u32[]{:S(2)}) %all-to-all-start) | async-done | bytes 65568 | tf_op jit(solution)/shard_map/all_to_all | solution.py:217
  29.3 0.1 broadcast_in_dim.20
  29.4 22.6 %all_to_all.30 = bf16[16,16,8,256]{3,2,1,0:T(8,128)(2,1)S(1)} all-to-all(bf16[16,16,8,256]{3,2,1,0:T(8,128)(2,1)S(1)} %broadcast_in_dim.20), channel_id=1, replica_groups=mesh['y'=4,'zl'=4,'x'=4,'zh'=4,'core'=2] {'x','y'}, dimensions={0} | all-to-all | bytes 2097152 | tf_op jit(solution)/shard_map/all_to_all | solution.py:217
  52.0 0.0 copy-start.1
  52.0 0.0 copy-start.2
  52.0 2.0 %collective-permute-start = (bf16[2048,256]{1,0:T(8,128)(2,1)S(1)}, bf16[2048,256]{1,0:T(8,128)(2,1)S(1)}, u32[]{:S(2)}, u32[]{:S(2)}) collective-permute-start(bf16[2048,256]{1,0:T(8,128)(2,1)S(1)} %bitcast.25), channel_id=1, source_target_pairs={{0,1},{1,0},{2,3},{3,2},{4,5},{5,4},{6,7},{7,6},{8,9},{9,8},{10,11... | collective-permute-start | bytes 3145736 | tf_op jit(solution)/shard_map/ppermute | solution.py:226
  54.1 0.5 fusion.1.mine_ref
  54.6 2.1 %collective-permute-done = bf16[2048,256]{1,0:T(8,128)(2,1)S(1)} collective-permute-done((bf16[2048,256]{1,0:T(8,128)(2,1)S(1)}, bf16[2048,256]{1,0:T(8,128)(2,1)S(1)}, u32[]{:S(2)}, u32[]{:S(2)}) %collective-permute-start) | collective-permute-done | bytes 1048608 | tf_op jit(solution)/shard_map/ppermute | solution.py:226
  56.7 0.5 fusion.2.other_ref
  57.2 0.0 copy-done.1
  57.2 0.0 copy-done.2
  57.2 0.2 shard_map.94
  57.4 39.0 %all_to_all.31.sent_ref = bf16[64,4,2816]{2,1,0:T(4,128)(2,1)S(1)} all-to-all(bf16[64,4,2816]{2,1,0:T(4,128)(2,1)S(1)} %shard_map.94), channel_id=1, replica_groups=mesh['y'=4,'zl'=4,'x'=4,'zh'=4,'core'=2] {'zl','x','y'}, dimensions={0} | all-to-all | bytes 2883584 | tf_op jit(solution)/shard_map/all_to_all | solution.py:217
  96.3 6.2 %shard_map.95 = bf16[64,4,2816]{2,1,0:T(4,128)(2,1)S(1)} custom-call(s32[4]{0:T(128)S(1)} %select_reduce_fusion.begin_ref, s32[1]{0:T(128)} %bitcast.3.first_ref, bf16[64,4,2816]{2,1,0:T(4,128)(2,1)S(1)} %all_to_all.31.sent_ref), custom_call_target="tpu_custom_call" | custom-call | flops 2013265920 | bytes 2883584 | tf_op jit(solution)/shard_map/pallas_call | solution.py:123
  102.6 41.7 %all_to_all.32.back_ref = bf16[64,4,2816]{2,1,0:T(4,128)(2,1)S(1)} all-to-all(bf16[64,4,2816]{2,1,0:T(4,128)(2,1)S(1)} %shard_map.95), channel_id=1, replica_groups=mesh['y'=4,'zl'=4,'x'=4,'zh'=4,'core'=2] {'zl','x','y'}, dimensions={0} | all-to-all | bytes 2883584 | tf_op jit(solution)/shard_map/all_to_all | solution.py:217
  144.3 0.1 shard_map.96
  144.3 0.4 convolution_convert_fusion
  144.8 1.9 collective-permute-start.1
  146.7 2.6 %collective-permute-done.1 = bf16[2048,256]{1,0:T(8,128)(2,1)S(1)} collective-permute-done((bf16[2048,256]{1,0:T(8,128)(2,1)S(1)}, bf16[2048,256]{1,0:T(8,128)(2,1)S(1)}, u32[]{:S(2)}, u32[]{:S(2)}) %collective-permute-start.1) | collective-permute-done | bytes 1048608 | tf_op jit(solution)/shard_map/ppermute | solution.py:226
  149.3 0.4 add_convert_fusion
  149.8 23.4 %all_to_all.33 = bf16[16,128,256]{2,1,0:T(8,128)(2,1)S(1)} all-to-all(bf16[16,128,256]{2,1,0:T(8,128)(2,1)S(1)} %bitcast.24), channel_id=1, replica_groups=mesh['y'=4,'zl'=4,'x'=4,'zh'=4,'core'=2] {'x','y'}, dimensions={0} | all-to-all | bytes 2097152 | tf_op jit(solution)/shard_map/all_to_all | solution.py:217
  173.2 0.8 convert_reduce_fusion
  174.0 5.8 %all-to-all-start.5 = ((f32[16,8,256]{2,1,0:T(8,128)}), f32[16,8,256]{2,1,0:T(8,128)S(1)}, u32[]{:S(2)}, u32[]{:S(2)}) async-start(f32[16,8,256]{2,1,0:T(8,128)} %bitcast.10), calls=%async_computation.5 | async-start | bytes 262144 | tf_op jit(solution)/shard_map/all_to_all | solution.py:217
  179.8 0.3 reshape.61
  180.2 1.1 slice_bitcast_fusion
  181.3 12.0 %all-to-all-done.5 = f32[16,8,256]{2,1,0:T(8,128)S(1)} async-done(((f32[16,8,256]{2,1,0:T(8,128)}), f32[16,8,256]{2,1,0:T(8,128)S(1)}, u32[]{:S(2)}, u32[]{:S(2)}) %all-to-all-start.5) | async-done | bytes 131104 | tf_op jit(solution)/shard_map/all_to_all | solution.py:217
  193.3 0.6 fusion
  (2 shorter events, 0.0 us)
Async XLA Ops:
  2.0 27.4 %all-to-all-start = ((bf16[16,8,256]{2,1,0:T(8,128)(2,1)}), bf16[16,8,256]{2,1,0:T(8,128)(2,1)S(1)}, u32[]{:S(2)}, u32[]{:S(2)}) async-start(bf16[16,8,256]{2,1,0:T(8,128)(2,1)} %broadcast_in_dim.18), calls=%async_computation | async-start | bytes 131072 | tf_op jit(solution)/shard_map/all_to_all | solution.py:217
  18.2 1.6 copy-start
  52.0 5.2 %copy-start.1 = (bf16[1,256,1024]{2,1,0:T(8,128)(2,1)S(1)}, bf16[1,256,1024]{2,1,0:T(8,128)(2,1)}, u32[]{:S(2)}) copy-start(bf16[1,256,1024]{2,1,0:T(8,128)(2,1)} %param.7) | copy-start | bytes 1572868
  52.0 5.2 %copy-start.2 = (bf16[1,256,1024]{2,1,0:T(8,128)(2,1)S(1)}, bf16[1,256,1024]{2,1,0:T(8,128)(2,1)}, u32[]{:S(2)}) copy-start(bf16[1,256,1024]{2,1,0:T(8,128)(2,1)} %param.8) | copy-start | bytes 1572868
  52.0 4.7 %collective-permute-start = (bf16[2048,256]{1,0:T(8,128)(2,1)S(1)}, bf16[2048,256]{1,0:T(8,128)(2,1)S(1)}, u32[]{:S(2)}, u32[]{:S(2)}) collective-permute-start(bf16[2048,256]{1,0:T(8,128)(2,1)S(1)} %bitcast.25), channel_id=1, source_target_pairs={{0,1},{1,0},{2,3},{3,2},{4,5},{5,4},{6,7},{7,6},{8,9},{9,8},{10,11... | collective-permute-start | bytes 3145736 | tf_op jit(solution)/shard_map/ppermute | solution.py:226
  144.8 4.6 %collective-permute-start.1 = (bf16[2048,256]{1,0:T(8,128)(2,1)S(1)}, bf16[2048,256]{1,0:T(8,128)(2,1)S(1)}, u32[]{:S(2)}, u32[]{:S(2)}) collective-permute-start(bf16[2048,256]{1,0:T(8,128)(2,1)S(1)} %convolution_convert_fusion), channel_id=1, source_target_pairs={{0,1},{1,0},{2,3},{3,2},{4,5},{5,4},{6,7},{7,6},{8,9},{9,8},{10,11... | collective-permute-start | bytes 3145736 | tf_op jit(solution)/shard_map/ppermute | solution.py:226
  174.0 19.3 %all-to-all-start.5 = ((f32[16,8,256]{2,1,0:T(8,128)}), f32[16,8,256]{2,1,0:T(8,128)S(1)}, u32[]{:S(2)}, u32[]{:S(2)}) async-start(f32[16,8,256]{2,1,0:T(8,128)} %bitcast.10), calls=%async_computation.5 | async-start | bytes 262144 | tf_op jit(solution)/shard_map/all_to_all | solution.py:217
